TPU v7x, 256 devices: a whole 4x4x8 slice. The times are simulated.
256 devices in a mesh: ctx: 32 (over z_lo, x, y), tp: 4 (over z_hi), grp: 2 (over core).
Axes of the slice: x: 4, y: 4, z: 8 (z_hi: 4, z_lo: 2; z = z_hi * 2 + z_lo), core: 2. Of those that a mesh axis runs over, the one named last changes fastest.
Arguments:
- new_queries: bfloat16 [2048, 8, 1024], P('ctx', ('tp', 'grp')), may hold values from -8 to 8
- new_keys: bfloat16 [2048, 8, 128], P('ctx', ('tp', 'grp')), may hold values from -6 to 6
- new_values: bfloat16 [2048, 8, 128], P('ctx', ('tp', 'grp')), may hold values from -6 to 6
- cached_keys: bfloat16 [32768, 8, 128], P('ctx', ('tp', 'grp')), may hold values from -6 to 6
- cached_values: bfloat16 [32768, 8, 128], P('ctx', ('tp', 'grp')), may hold values from -6 to 6
- decode_queries: bfloat16 [128, 8, 1024], P('ctx', 'grp'), may hold values from -8 to 8
- decode_keys: bfloat16 [128, 2048, 8, 128], P('ctx', 'tp', 'grp'), may hold values from -6 to 6
- decode_values: bfloat16 [128, 2048, 8, 128], P('ctx', 'tp', 'grp'), may hold values from -6 to 6
- decode_lengths: int32 [128], P('ctx'), may hold values from 256 to 2048, as said below
- source_block: int32 [128], P('ctx'), may hold values from 0 to 31
Outputs:
- prefill_out: bfloat16 [2048, 8, 1024], P('ctx', ('tp', 'grp'))
- decode_out: bfloat16 [128, 8, 1024], P('ctx', 'grp')
Inputs may be any that keep to these rules, and one draw needn't show every extreme that they name: `decode_lengths`: some decode row has all 2048 positions live.
All inputs are finite; a program needn't handle non-finite values.
Results may differ from a plain program's by a relative error of at most 0.0015.
Values may be sent and summed in bfloat16 or wider, within the bound.
No kernel may reach another device: no remote copies, remote signals or barrier semaphores. Data moves between devices by JAX's collectives and lax.ppermute only.
A program may use at most 128 MiB of HBM per device.

v0:
```python
import math

import jax
import jax.numpy as jnp
from jax import lax
from jax.sharding import PartitionSpec as P

neg_fill = -1e30


def merged(part, axis, combine):
    gathered = jax.tree.map(lambda a: lax.all_gather(a, axis), part)

    def take(source):
        return jax.tree.map(lambda a: lax.dynamic_index_in_dim(a, source, 0, False), gathered)

    return lax.fori_loop(
        1, lax.axis_size(axis), lambda source, state: combine(state, take(source)), take(0)
    )


def attend_keys(state_in, queries, key_rows, value_rows, row_tokens):
    key_count = key_rows.shape[0]
    block_width = math.gcd(key_count, 1024)
    block_count = key_count // block_width
    scale_factor = queries.shape[2] ** (-0.5)
    key_blocks = key_rows.reshape(block_count, block_width, key_rows.shape[1], key_rows.shape[2])
    value_blocks = value_rows.reshape(
        block_count, block_width, value_rows.shape[1], value_rows.shape[2]
    )
    offsets = jnp.arange(block_count, dtype=jnp.int32) * block_width

    def one_block(state_now, pieces):
        out_acc, run_max, run_sum = state_now
        key_block, value_block, offset = pieces
        scores = (
            jnp.einsum("hrd,nhd->hrn", queries, key_block, preferred_element_type=jnp.float32)
            * scale_factor
        )
        if row_tokens is None:
            new_max = jnp.maximum(run_max, jnp.max(scores, axis=2))
            weights = jnp.exp(scores - new_max[:, :, None])
        else:
            allowed = (offset + jnp.arange(block_width, dtype=jnp.int32))[None, :] <= row_tokens[
                :, None
            ]
            scores = jnp.where(allowed[None], scores, neg_fill)
            new_max = jnp.maximum(run_max, jnp.max(scores, axis=2))
            weights = jnp.where(allowed[None], jnp.exp(scores - new_max[:, :, None]), 0.0)
        factor = jnp.exp(run_max - new_max)
        run_sum = run_sum * factor + jnp.sum(weights, axis=2)
        out_acc = out_acc * factor[:, :, None] + jnp.einsum(
            "hrn,nhd->hrd",
            weights,
            value_block.astype(jnp.float32),
            precision=lax.Precision.HIGHEST,
        )
        return ((out_acc, new_max, run_sum), None)

    result, unused = lax.scan(one_block, state_in, (key_blocks, value_blocks, offsets))
    return result


def merge_parts(earlier, later):
    top_score = jnp.maximum(earlier[1], later[1])
    factor_one = jnp.exp(earlier[1] - top_score)
    factor_two = jnp.exp(later[1] - top_score)
    out_acc = earlier[0] * factor_one[..., None] + later[0] * factor_two[..., None]
    return (out_acc, top_score, earlier[2] * factor_one + later[2] * factor_two)


def local(
    new_queries,
    new_keys,
    new_values,
    cached_keys,
    cached_values,
    decode_queries,
    decode_keys,
    decode_values,
    decode_lengths,
    source_block,
):
    new_dev, heads_here, wide_rows = new_queries.shape
    head_dim = new_keys.shape[2]
    groups = wide_rows // head_dim
    block_index = lax.axis_index("ctx")
    count_now = new_queries.shape[0]
    shaped = new_queries.reshape(count_now, heads_here, groups, head_dim).transpose(1, 0, 2, 3)
    own_queries = shaped.reshape(heads_here, count_now * groups, head_dim)
    row_count = new_dev * groups
    pieces = (
        lax.all_gather(cached_keys, "ctx", axis=0, tiled=True),
        lax.all_gather(cached_values, "ctx", axis=0, tiled=True),
    )
    state_now = attend_keys(
        (
            jnp.zeros((heads_here, row_count, head_dim), jnp.float32),
            jnp.full((heads_here, row_count), neg_fill, jnp.float32),
            jnp.zeros((heads_here, row_count), jnp.float32),
        ),
        own_queries,
        pieces[0],
        pieces[1],
        None,
    )
    row_tokens = block_index * new_dev + jnp.arange(row_count, dtype=jnp.int32) // groups
    pieces = (
        lax.all_gather(new_keys, "ctx", axis=0, tiled=True),
        lax.all_gather(new_values, "ctx", axis=0, tiled=True),
    )
    state_now = attend_keys(state_now, own_queries, pieces[0], pieces[1], row_tokens)
    prefill_rows = state_now[0] / state_now[2][:, :, None]
    prefill_out = (
        prefill_rows.reshape(heads_here, new_dev, groups * head_dim)
        .transpose(1, 0, 2)
        .astype(jnp.bfloat16)
    )
    rows_dev, dec_heads, unused_width = decode_queries.shape
    part_len = decode_keys.shape[1]
    tp_index = lax.axis_index("tp")
    grp_index = lax.axis_index("grp")
    piece_len = new_dev // lax.axis_size("tp")
    blocks = (
        lax.all_gather(new_keys, "ctx", axis=0, tiled=True),
        lax.all_gather(new_values, "ctx", axis=0, tiled=True),
    )
    blocks = (
        lax.all_gather(blocks[0], ("tp", "grp"), axis=1, tiled=True),
        lax.all_gather(blocks[1], ("tp", "grp"), axis=1, tiled=True),
    )

    def pick_rows(array_in):
        count_blocks = array_in.shape[0] // new_dev
        shaped = array_in.reshape(count_blocks, new_dev, array_in.shape[1], head_dim)
        shaped = lax.dynamic_slice_in_dim(shaped, tp_index * piece_len, piece_len, 1)
        return lax.dynamic_slice_in_dim(shaped, grp_index * dec_heads, dec_heads, 2)

    handed = (pick_rows(blocks[0]), pick_rows(blocks[1]))
    hand_keys = jnp.take(handed[0], source_block, axis=0)
    hand_values = jnp.take(handed[1], source_block, axis=0)
    scale_factor = head_dim ** (-0.5)
    dec_query = decode_queries.reshape(rows_dev, dec_heads, groups, head_dim)
    cache_scores = (
        jnp.einsum("bhgd,bshd->bhgs", dec_query, decode_keys, preferred_element_type=jnp.float32)
        * scale_factor
    )
    positions = tp_index * part_len + jnp.arange(part_len, dtype=jnp.int32)
    live_mask = (positions[None, :] < decode_lengths[:, None])[:, None, None, :]
    cache_scores = jnp.where(live_mask, cache_scores, neg_fill)
    hand_scores = (
        jnp.einsum("bhgd,bshd->bhgs", dec_query, hand_keys, preferred_element_type=jnp.float32)
        * scale_factor
    )
    top_score = jnp.maximum(jnp.max(cache_scores, axis=3), jnp.max(hand_scores, axis=3))
    cache_weights = jnp.where(live_mask, jnp.exp(cache_scores - top_score[..., None]), 0.0)
    hand_weights = jnp.exp(hand_scores - top_score[..., None])
    total_w = jnp.sum(cache_weights, axis=3) + jnp.sum(hand_weights, axis=3)
    out_acc = jnp.einsum(
        "bhgs,bshd->bhgd",
        cache_weights,
        decode_values.astype(jnp.float32),
        precision=lax.Precision.HIGHEST,
    )
    out_acc = out_acc + jnp.einsum(
        "bhgs,bshd->bhgd",
        hand_weights,
        hand_values.astype(jnp.float32),
        precision=lax.Precision.HIGHEST,
    )
    out_acc, top_score, total_w = merged((out_acc, top_score, total_w), "tp", merge_parts)
    decode_out = (
        (out_acc / total_w[..., None])
        .reshape(rows_dev, dec_heads, groups * head_dim)
        .astype(jnp.bfloat16)
    )
    return (prefill_out, decode_out)


def solution(mesh):
    in_specs = (
        P("ctx", ("tp", "grp"), None),
        P("ctx", ("tp", "grp"), None),
        P("ctx", ("tp", "grp"), None),
        P("ctx", ("tp", "grp"), None),
        P("ctx", ("tp", "grp"), None),
        P("ctx", "grp", None),
        P("ctx", "tp", "grp", None),
        P("ctx", "tp", "grp", None),
        P("ctx"),
        P("ctx"),
    )
    out_specs = (P("ctx", ("tp", "grp"), None), P("ctx", "grp", None))
    return jax.shard_map(local, mesh=mesh, in_specs=in_specs, out_specs=out_specs, check_vma=False)
```

profile of v0, /device:TPU:8, one launch (start us, length us, event | category | flops | bytes accessed | tf_op | source)
XLA Modules:
  0.0 850.7 jit_solution(5861043292157205514)
XLA Ops:
  7.3 85.4 %all_gather.37 = bf16[2048,1,128]{2,0,1:T(8,128)(2,1)} all-gather(bf16[64,1,128]{2,0,1:T(8,128)(2,1)} %param.20), channel_id=1, replica_groups=mesh['ctx'=32,'tp'=4,'grp'=2] {'ctx'}, dimensions={0}, use_global_device_ids=true | all-gather | bytes 540672 | tf_op jit(solution)/shard_map/all_gather | solution.py:110
  92.8 95.1 %all_gather.36 = bf16[2048,1,128]{2,0,1:T(8,128)(2,1)} all-gather(bf16[64,1,128]{2,0,1:T(8,128)(2,1)} %param.19), channel_id=1, replica_groups=mesh['ctx'=32,'tp'=4,'grp'=2] {'ctx'}, dimensions={0}, use_global_device_ids=true | all-gather | bytes 540672 | tf_op jit(solution)/shard_map/all_gather | solution.py:109
  190.3 49.0 %all-gather.12.cloned.1.call-done = bf16[2048,8,128]{2,0,1:T(8,128)(2,1)} async-done(((bf16[2048,1,128]{2,0,1:T(8,128)(2,1)}), bf16[2048,8,128]{2,0,1:T(8,128)(2,1)}) %all-gather.12.cloned.1.call-update) | async-done | bytes 4194320 | tf_op jit(solution)/shard_map/all_gather | solution.py:129
  247.3 14.3 %all-gather = f32[16,4,8,128]{3,2,1,0:T(8,128)S(1)} all-gather(f32[4,4,8,128]{3,2,1,0:T(8,128)S(1)} %convolution_add_fusion), channel_id=2, replica_groups=mesh['ctx'=32,'tp'=4,'grp'=2] {'tp'}, dimensions={0}, use_global_device_ids=true | all-gather | bytes 327680 | tf_op jit(solution)/shard_map/all_gather | solution.py:12
  261.7 13.7 %all-gather.1 = f32[16,4,8]{2,1,0:T(4,128)S(1)} all-gather(f32[4,4,8]{2,1,0:T(4,128)S(1)} %max.33), channel_id=3, replica_groups=mesh['ctx'=32,'tp'=4,'grp'=2] {'tp'}, dimensions={0}, use_global_device_ids=true | all-gather | bytes 2560 | tf_op jit(solution)/shard_map/all_gather | solution.py:12
  275.8 13.7 %all-gather.2 = f32[16,4,8]{2,1,0:T(4,128)S(1)} all-gather(f32[4,4,8]{2,1,0:T(4,128)S(1)} %add.147), channel_id=4, replica_groups=mesh['ctx'=32,'tp'=4,'grp'=2] {'tp'}, dimensions={0}, use_global_device_ids=true | all-gather | bytes 2560 | tf_op jit(solution)/shard_map/all_gather | solution.py:12
  290.7 119.8 %all-gather.8.cloned.1.call-done = bf16[32768,1,128]{2,0,1:T(8,128)(2,1)} async-done(((bf16[1024,1,128]{2,0,1:T(8,128)(2,1)}), bf16[32768,1,128]{2,0,1:T(8,128)(2,1)}) %all-gather.8.cloned.1.call-update) | async-done | bytes 8388624 | tf_op jit(solution)/shard_map/all_gather | solution.py:93
  410.6 172.7 %all-gather.10.cloned.1.call-done = bf16[32768,1,128]{2,0,1:T(8,128)(2,1)} async-done(((bf16[1024,1,128]{2,0,1:T(8,128)(2,1)}), bf16[32768,1,128]{2,0,1:T(8,128)(2,1)}) %all-gather.10.cloned.1.call-update) | async-done | bytes 8388624 | tf_op jit(solution)/shard_map/all_gather | solution.py:94
  583.3 250.9 %while.51 = (s32[]{:T(128)}, f32[1,512,128]{2,1,0:T(8,128)S(1)}, f32[1,512]{1,0:T(1,128)S(1)}, f32[1,512]{1,0:T(1,128)S(1)}, bf16[32,1024,1,128]{3,1,2,0:T(8,128...) while((s32[]{:T(128)}, f32[1,512,128]{2,1,0:T(8,128)S(1)}, ...), condition=%wide.region_3.4_spmd.clone, body=%wide.region_0.3_spmd.clone.sunk | while | flops 943393280 | bytes 15892629 | solution.py:60
  583.3 2.8 multiply_reduce_fusion.2
  588.3 2.9 fusion.103
  591.2 2.7 multiply_reduce_fusion.2
  596.1 2.9 fusion.103
  604.0 2.9 fusion.103
  611.8 2.9 fusion.103
  614.7 2.7 multiply_reduce_fusion.2
  619.7 2.9 fusion.103
  627.5 2.9 fusion.103
  635.3 2.9 fusion.103
  638.2 2.7 multiply_reduce_fusion.2
  643.2 2.9 fusion.103
  651.0 2.9 fusion.103
  658.9 2.9 fusion.103
  661.7 2.7 multiply_reduce_fusion.2
  666.7 2.9 fusion.103
  674.5 2.9 fusion.103
  682.4 2.9 fusion.103
  685.3 2.7 multiply_reduce_fusion.2
  690.2 2.9 fusion.103
  698.1 2.9 fusion.103
  705.9 2.9 fusion.103
  713.7 2.9 fusion.103
  721.6 2.9 fusion.103
  729.4 2.9 fusion.103
  737.3 2.9 fusion.103
  745.1 2.9 fusion.103
  752.9 2.9 fusion.103
  760.8 2.9 fusion.103
  768.6 2.9 fusion.103
  776.5 2.9 fusion.103
  784.3 2.9 fusion.103
  792.1 2.9 fusion.103
  800.0 2.9 fusion.103
  807.8 2.9 fusion.103
  815.7 2.9 fusion.103
  823.5 2.9 fusion.103
  831.3 2.9 fusion.103
  834.2 9.1 %while.50 = (s32[]{:T(128)}, f32[1,512,128]{2,1,0:T(8,128)S(1)}, f32[1,512]{1,0:T(1,128)S(1)}, f32[1,512]{1,0:T(1,128)S(1)}, s32[2]{0:T(128)S(1)}, /*index=5*/bf...) while((s32[]{:T(128)}, f32[1,512,128]{2,1,0:T(8,128)S(1)}, ...), condition=%wide.region_7.8_spmd.clone, body=%wide.region_4.7_spmd.clone.sunk | while | flops 947526144 | bytes 7528585 | solution.py:60
  (295 shorter events, 164.3 us)
Async XLA Ops:
  7.2 182.4 %copy-start = (bf16[4,512,4,128]{3,2,1,0:T(4,128)(2,1)S(1)}, bf16[4,512,4,128]{3,2,1,0:T(4,128)(2,1)}, u32[]{:S(2)}) copy-start(bf16[4,512,4,128]{3,2,1,0:T(4,128)(2,1)} %param.24) | copy-start | bytes 6291460
  7.2 182.1 %copy-start.4 = (bf16[64,1,1024]{2,0,1:T(8,128)(2,1)S(1)}, bf16[64,1,1024]{2,0,1:T(8,128)(2,1)}, u32[]{:S(2)}) copy-start(bf16[64,1,1024]{2,0,1:T(8,128)(2,1)} %param.18) | copy-start | bytes 393220
  7.2 182.2 %copy-start.5 = (bf16[4,4,1024]{2,1,0:T(4,128)(2,1)S(1)}, bf16[4,4,1024]{2,1,0:T(4,128)(2,1)}, u32[]{:S(2)}) copy-start(bf16[4,4,1024]{2,1,0:T(4,128)(2,1)} %param.23) | copy-start | bytes 98308
  7.2 182.2 %copy-start.7 = (s32[4]{0:T(128)S(1)}, s32[4]{0:T(128)}, u32[]{:S(2)}) copy-start(s32[4]{0:T(128)} %param.27) | copy-start | bytes 52
  7.2 182.3 %copy-start.6 = (s32[4]{0:T(128)S(1)}, s32[4]{0:T(128)}, u32[]{:S(2)}) copy-start(s32[4]{0:T(128)} %param.26) | copy-start | bytes 52
  7.2 183.1 %all-gather.14.cloned.1.call-start = ((), (), s32[]{:S(2)}) async-start(), calls=%async_computation.3 | async-start | bytes 4718592 | tf_op jit(solution)/shard_map/all_gather | solution.py:130
  92.7 146.6 %all-gather.12.cloned.1.call-start = ((), (), s32[]{:S(2)}) async-start(), calls=%async_computation.2 | async-start | bytes 4718592 | tf_op jit(solution)/shard_map/all_gather | solution.py:129
  187.9 222.6 %all-gather.8.cloned.1.call-start = ((), (), s32[]{:S(2)}) async-start(), calls=%async_computation | async-start | bytes 8650752 | tf_op jit(solution)/shard_map/all_gather | solution.py:93
  188.7 394.6 %all-gather.10.cloned.1.call-start = ((), (), s32[]{:S(2)}) async-start(), calls=%async_computation.1 | async-start | bytes 8650752 | tf_op jit(solution)/shard_map/all_gather | solution.py:94
  583.2 251.0 %copy-start.2 = (bf16[2048,1,128]{2,0,1:T(8,128)(2,1)S(1)}, bf16[2048,1,128]{2,0,1:T(8,128)(2,1)}, u32[]{:S(2)}) copy-start(bf16[2048,1,128]{2,0,1:T(8,128)(2,1)} %all_gather.37) | copy-start | bytes 1572868
  583.3 251.0 %copy-start.3 = (bf16[2048,1,128]{2,0,1:T(8,128)(2,1)S(1)}, bf16[2048,1,128]{2,0,1:T(8,128)(2,1)}, u32[]{:S(2)}) copy-start(bf16[2048,1,128]{2,0,1:T(8,128)(2,1)} %all_gather.36) | copy-start | bytes 1572868
  586.1 2.2 copy-start.1
  593.9 2.2 copy-start.1
  601.8 2.2 copy-start.1
  609.6 2.2 copy-start.1
  617.4 2.2 copy-start.1
  625.3 2.2 copy-start.1
  633.1 2.2 copy-start.1
  641.0 2.2 copy-start.1
  648.8 2.2 copy-start.1
  656.6 2.2 copy-start.1
  664.5 2.2 copy-start.1
  672.3 2.2 copy-start.1
  680.1 2.2 copy-start.1
  688.0 2.2 copy-start.1
  695.8 2.2 copy-start.1
  703.7 2.2 copy-start.1
  711.5 2.2 copy-start.1
  719.4 2.2 copy-start.1
  727.2 2.2 copy-start.1
  735.0 2.2 copy-start.1
  742.9 2.2 copy-start.1
  750.7 2.2 copy-start.1
  758.5 2.2 copy-start.1
  766.4 2.2 copy-start.1
  774.2 2.2 copy-start.1
  782.1 2.2 copy-start.1
  789.9 2.2 copy-start.1
  797.7 2.2 copy-start.1
  805.6 2.2 copy-start.1
  813.4 2.2 copy-start.1
  821.3 2.2 copy-start.1
  829.1 2.2 copy-start.1
Sparse Core Ops, SparseCore 0:
  92.8 54.2 all-gather.13
  188.1 51.1 all-gather.11
  241.1 169.4 all-gather.7
  412.2 171.0 all-gather.9
where the time goes:
time: 853 us; the launch traced here: 851 us
  waiting for transfers between devices  343 us (40%)
  blocking collectives  222 us (26%)
  matrix products  188 us (22%)
  other arithmetic  72.8 us (9%)
  between operations  14 us (2%)
  local copies, waits for them, and re-layouts  9.3 us (1%)
    all_gather x1, waiting for transfers between devices, local(): lax.all_gather(cached_values, 'ctx', axis=0, tiled=True)  173 us
    all_gather x1, waiting for transfers between devices, local(): lax.all_gather(cached_keys, 'ctx', axis=0, tiled=True)  120 us
    dot_general x34, matrix products, one_block(): jnp.einsum('hrn,nhd->hrd', weights, value_block.astype(jnp.float32), prec...  95.7 us
    all_gather x1, blocking collectives, local(): lax.all_gather(new_keys, 'ctx', axis=0, tiled=True)  95.1 us
    dot_general x34, matrix products, one_block(): jnp.einsum('hrd,nhd->hrn', queries, key_block, preferred_element_type=jnp...  88.5 us
    all_gather x1, blocking collectives, local(): lax.all_gather(new_values, 'ctx', axis=0, tiled=True)  85.4 us
    reduce_sum x34, other arithmetic, one_block(): run_sum = run_sum * factor + jnp.sum(weights, axis=2)  69.7 us
    all_gather x1, waiting for transfers between devices, local(): lax.all_gather(blocks[0], ('tp', 'grp'), axis=1, tiled=True)  49 us
  transfers between devices with their start and end apart: 4, of which 3 were waited for; matrix products, arithmetic and copies ran while one was open for 1% of the time, Pallas kernels for 0%

commit v1 on v0

v1 whole, which is shorter than its diff:
```python
import functools
import math

import jax
import jax.numpy as jnp
from jax import lax
from jax.experimental import pallas as pl
from jax.experimental.pallas import tpu as pltpu
from jax.sharding import PartitionSpec as P

f32 = jnp.float32
bf16 = jnp.bfloat16
i16 = jnp.int16
i32 = jnp.int32

HD = 128
GROUPS = 8
TOK = 64
CACHE = 1024
QS = 8
KS = 4
NEWK = KS * TOK
SCALE2 = HD**-0.5 * math.log2(math.e)
NEG = -1e30
NOTHING = -1000.0
CODE = 32767.0
MESSAGE = 144
VMEM_LIMIT = 56 * 2**20


def contract_last(a, b):
    return lax.dot_general(a, b, (((1,), (1,)), ((), ())), preferred_element_type=f32)


def matmul(a, b):
    return jnp.dot(a, b, preferred_element_type=f32)


def split(p):
    high = p.astype(bf16)
    return high, (p - high.astype(f32)).astype(bf16)


def two_words(x):
    big = jnp.round(x * 32.0)
    return big, jnp.round((x * 32.0 - big) * 32768.0)


def one_number(big, small):
    return (big + small * (1.0 / 32768.0)) * (1.0 / 32.0)


def prefill_kernel(*refs):
    meta = refs[0]
    queries = refs[1 : 1 + QS]
    pairs = refs[1 + QS : 1 + QS + KS]
    outs = refs[1 + QS + KS : 1 + 2 * QS + KS]
    q_all, new_keys, values_t, out_t, lse_all = refs[1 + 2 * QS + KS :]
    for s in range(QS):
        q_all[s] = queries[s][...]
    for j in range(KS):
        new_keys[j * TOK : (j + 1) * TOK, :] = pairs[j][CACHE : CACHE + TOK, :]
        values_t[:, j * CACHE : (j + 1) * CACHE] = pairs[j][CACHE + TOK : 2 * CACHE + TOK, :].T
    new_values = jnp.concatenate([pairs[j][2 * CACHE + TOK :, :] for j in range(KS)], 0)
    values_t[:, KS * CACHE :] = new_values.T

    def keys_of(i):
        return pairs[i][:CACHE, :] if i < KS else new_keys[...]

    def values_of(i):
        return values_t[:, i * CACHE : min((i + 1) * CACHE, KS * CACHE + NEWK)]

    def tile_queries(b, half):
        start = half * (4 * HD)
        return jnp.concatenate(
            [q_all[b, :, start + g * HD : start + (g + 1) * HD] for g in range(4)], 0
        )

    def allowed(b):
        offset = lax.broadcasted_iota(i32, (TOK, 4 * TOK), 0)
        token = lax.broadcasted_iota(i32, (TOK, 4 * TOK), 1) & (TOK - 1)
        limit = token + meta[b] * TOK
        return jnp.concatenate(
            [offset + meta[QS + j] * TOK <= limit for j in range(KS)], 0
        )

    def put(b, half, total, acc):
        lanes = slice(half * 4 * TOK, (half + 1) * 4 * TOK)
        out_t[b, :, lanes] = acc / total
        lse_all[b, 0:1, lanes] = jnp.log2(total)

    def one_block(b, carry):
        mask = allowed(b)
        tiles = [tile_queries(b, half) for half in range(2)]
        sums = [jnp.zeros((8, 4 * TOK), f32) for unused in range(2)]
        accs = [jnp.zeros((HD, 4 * TOK), f32) for unused in range(2)]
        work = [(i, t) for i in range(KS + 1) for t in range(2)]
        following = contract_last(keys_of(0), tiles[0])
        for w, (i, t) in enumerate(work):
            scores = following
            if w + 1 < len(work):
                following = contract_last(keys_of(work[w + 1][0]), tiles[work[w + 1][1]])
            weights = jnp.exp2(scores * SCALE2)
            if i == KS:
                weights = jnp.where(mask, weights, 0.0)
            sums[t] = sums[t] + jnp.sum(weights.reshape(-1, 8, 4 * TOK), 0)
            high, low = split(weights)
            accs[t] = accs[t] + matmul(values_of(i), high) + matmul(values_of(i), low)
        for t in range(2):
            put(b, t, jnp.sum(sums[t], 0, keepdims=True), accs[t])
        return carry

    lax.fori_loop(0, QS, one_block, 0)

    lse = lse_all[:, 0, :]
    fine = jnp.where((lse > -60.0) & (lse < 100.0), 0, 1)

    @pl.when(jnp.max(fine) > 0)
    def again():
        def one(b, carry):
            mask = allowed(b)
            for t in range(2):
                tile = tile_queries(b, t)
                top = jnp.full((1, 4 * TOK), NEG, f32)
                total = jnp.zeros((1, 4 * TOK), f32)
                acc = jnp.zeros((HD, 4 * TOK), f32)
                for i in range(KS + 1):
                    scores = contract_last(keys_of(i), tile) * SCALE2
                    if i == KS:
                        scores = jnp.where(mask, scores, NEG)
                    new_top = jnp.maximum(top, jnp.max(scores, 0, keepdims=True))
                    weights = jnp.exp2(scores - new_top)
                    factor = jnp.exp2(top - new_top)
                    total = total * factor + jnp.sum(weights, 0, keepdims=True)
                    high, low = split(weights)
                    acc = acc * factor + matmul(values_of(i), high) + matmul(values_of(i), low)
                    top = new_top
                put(b, t, total, acc)
                lanes = slice(t * 4 * TOK, (t + 1) * 4 * TOK)
                lse_all[b, 0:1, lanes] = jnp.log2(total) + top
            return carry

        lax.fori_loop(0, QS, one, 0)

    hand_q = jnp.concatenate([q_all[s, 0:32, 8 * HD :] for s in range(QS)], 0)
    source = jnp.concatenate([q_all[s, 32:64, 8 * HD :] for s in range(QS)], 0).astype(f32)
    lane = lax.broadcasted_iota(i32, (QS * 32, HD), 1)
    keep = jnp.concatenate(
        [
            source == jnp.where(lane < TOK, meta[QS + 2 * j], meta[QS + 2 * j + 1]).astype(f32)
            for j in range(2)
        ],
        1,
    )
    scores = jnp.where(keep, contract_last(hand_q, new_keys[...]) * SCALE2, NEG)
    top = jnp.max(scores, 1, keepdims=True)
    weights = jnp.where(keep, jnp.exp2(scores - top), 0.0)
    total = jnp.sum(weights, 1, keepdims=True)
    both = matmul(jnp.concatenate(split(weights), 0), new_values)
    some = total > 0.0
    hand = (both[: QS * 32] + both[QS * 32 :]) / jnp.where(some, total, 1.0)
    hand_lse = jnp.where(some, jnp.log2(jnp.where(some, total, 1.0)) + top, NOTHING)
    most = jnp.maximum(jnp.max(jnp.abs(hand), 1, keepdims=True), 1e-30)
    hand = hand * (CODE / most)
    wide_lse = jnp.broadcast_to(hand_lse, (QS * 32, HD))
    wide_most = jnp.broadcast_to(jnp.log2(most), (QS * 32, HD))
    row_lse = jnp.concatenate([wide_lse[:HD].T[0:8], wide_lse[HD:].T[0:8]], 1)
    row_most = jnp.concatenate([wide_most[:HD].T[0:8], wide_most[HD:].T[0:8]], 1)

    for s in range(QS):
        out = out_t[s]
        most_t = jnp.maximum(jnp.max(jnp.abs(out), 0, keepdims=True), 1e-30)
        outs[s][0:HD, :] = jnp.round(out * (CODE / most_t)).astype(i32).astype(i16)
        lse_words = two_words(lse_all[s, 0:1, :])
        most_words = two_words(jnp.log2(most_t))
        spare = jnp.zeros((1, 8 * TOK - 32), f32)
        lanes = slice(s * 32, (s + 1) * 32)
        small = [jnp.concatenate([row[0:1, lanes], spare], 1) for row in (row_lse, row_most)]
        words = [*two_words(small[0]), *two_words(small[1])]
        slab = jnp.concatenate([hand[s * 32 + 8 * k : s * 32 + 8 * k + 8] for k in range(4)], 1)
        rest = jnp.concatenate([*lse_words, *most_words, *words, jnp.round(slab)], 0)
        outs[s][HD:MESSAGE, :] = rest.astype(i32).astype(i16)


def prefill(meta, queries, pairs):
    vmem = pl.BlockSpec(memory_space=pltpu.VMEM)
    return pl.pallas_call(
        prefill_kernel,
        name="prefill",
        in_specs=[pl.BlockSpec(memory_space=pltpu.SMEM)] + [vmem] * (QS + KS),
        out_specs=[vmem] * QS,
        out_shape=[jax.ShapeDtypeStruct((MESSAGE, 8 * TOK), i16)] * QS,
        scratch_shapes=[
            pltpu.VMEM((QS, TOK, 9 * HD), bf16),
            pltpu.VMEM((NEWK, HD), bf16),
            pltpu.VMEM((HD, KS * CACHE + NEWK), bf16),
            pltpu.VMEM((QS, HD, 8 * TOK), f32),
            pltpu.VMEM((QS, 8, 8 * TOK), f32),
        ],
        compiler_params=pltpu.CompilerParams(vmem_limit_bytes=VMEM_LIMIT),
        cost_estimate=pl.CostEstimate(
            flops=6 * 4096 * 4352 * 128 * 2, bytes_accessed=4_000_000, transcendentals=4096 * 4352
        ),
    )(meta, *queries, *pairs)


def combine_kernel(*refs):
    parts = refs[:QS]
    out_ref, hand_ref = refs[QS:]
    tails = [part[HD:MESSAGE, :].astype(i32).astype(f32) for part in parts]
    lse = [one_number(tail[0:1], tail[1:2]) for tail in tails]
    most = [one_number(tail[2:3], tail[3:4]) for tail in tails]
    top = functools.reduce(jnp.maximum, lse)
    total = sum(jnp.exp2(x - top) for x in lse)
    acc = jnp.zeros((HD, 8 * TOK), f32)
    for s in range(QS):
        factor = jnp.exp2(lse[s] + most[s] - top) / (total * CODE)
        acc = acc + parts[s][0:HD, :].astype(i32).astype(f32) * factor
    rows = acc.T
    for g in range(GROUPS):
        out_ref[:, g * HD : (g + 1) * HD] = rows[g * TOK : (g + 1) * TOK].astype(bf16)
    small = jnp.concatenate(
        [tail[4:8, 0:HD] for tail in tails] + [jnp.zeros((HD - 4 * QS, HD), f32)], 0
    )
    columns = small.T[0:32]
    lse, most = [], []
    for s in range(QS):
        four = [columns[:, 4 * s + k : 4 * s + k + 1] for k in range(4)]
        lse.append(one_number(four[0], four[1]))
        most.append(one_number(four[2], four[3]))
    top = functools.reduce(jnp.maximum, lse)
    total = sum(jnp.exp2(x - top) for x in lse)
    hand = jnp.zeros((32, HD), f32)
    for s in range(QS):
        slab = jnp.concatenate([tails[s][8:16, k * HD : (k + 1) * HD] for k in range(4)], 0)
        hand = hand + slab * (jnp.exp2(lse[s] + most[s] - top) / (total * CODE))
    hand_ref[0:32] = hand
    hand_ref[32:64] = jnp.broadcast_to(jnp.log2(total) + top, (32, HD))


def combine(parts):
    return pl.pallas_call(
        combine_kernel,
        name="combine",
        out_shape=[
            jax.ShapeDtypeStruct((TOK, 8 * HD), bf16),
            jax.ShapeDtypeStruct((64, HD), f32),
        ],
        compiler_params=pltpu.CompilerParams(vmem_limit_bytes=VMEM_LIMIT),
        cost_estimate=pl.CostEstimate(flops=2_000_000, bytes_accessed=1_300_000, transcendentals=10_000),
    )(*parts)


def decode_kernel(meta, q_ref, k_ref, v_ref, out_ref):
    row = pl.program_id(0)
    scores = contract_last(q_ref[0], k_ref[0]) * SCALE2
    column = lax.broadcasted_iota(i32, scores.shape, 1)
    head = lax.broadcasted_iota(i32, scores.shape, 0) >> 3
    keep = ((column & 3) == head) & ((column >> 2) < meta[row])
    scores = jnp.where(keep, scores, NEG)
    top = jnp.max(scores, 1, keepdims=True)
    weights = jnp.where(keep, jnp.exp2(scores - top), 0.0)
    total = jnp.sum(weights, 1, keepdims=True)
    both = matmul(jnp.concatenate(split(weights), 0), v_ref[0])
    some = total > 0.0
    safe = jnp.where(some, total, 1.0)
    out_ref[0, 0:32] = (both[0:32] + both[32:64]) / safe
    out_ref[0, 32:64] = jnp.broadcast_to(
        jnp.where(some, jnp.log2(safe) + top, NOTHING), (32, HD)
    )


def decode_cache(live, queries, keys, values):
    rows, width, unused = keys.shape
    return pl.pallas_call(
        decode_kernel,
        name="decode_cache",
        grid=(rows,),
        in_specs=[
            pl.BlockSpec(memory_space=pltpu.SMEM),
            pl.BlockSpec((1, 32, HD), lambda r: (r, 0, 0)),
            pl.BlockSpec((1, width, HD), lambda r: (r, 0, 0)),
            pl.BlockSpec((1, width, HD), lambda r: (r, 0, 0)),
        ],
        out_specs=pl.BlockSpec((1, 64, HD), lambda r: (r, 0, 0)),
        out_shape=jax.ShapeDtypeStruct((rows, 64, HD), f32),
        compiler_params=pltpu.CompilerParams(vmem_limit_bytes=VMEM_LIMIT),
        cost_estimate=pl.CostEstimate(
            flops=200_000_000, bytes_accessed=4_400_000, transcendentals=262_144
        ),
    )(live, queries, keys, values)


def finish_kernel(*refs):
    meta = refs[0]
    parts = refs[1:5]
    hands = refs[5:9]
    out_ref, placed = refs[9:]
    for k in range(4):
        placed[meta[k]] = hands[k][...]
    for r in range(4):
        rows = slice(r * 8, r * 8 + 8)
        outs = [part[r, 0:32] for part in parts]
        lse = [part[r, 32:64] for part in parts]
        outs.append(jnp.concatenate([placed[j, rows] for j in range(4)], 0))
        lse.append(jnp.concatenate([placed[j, r * 8 + 32 : r * 8 + 40] for j in range(4)], 0))
        top = functools.reduce(jnp.maximum, lse)
        factors = [jnp.exp2(x - top) for x in lse]
        out_ref[r] = (sum(o * w for o, w in zip(outs, factors)) / sum(factors)).astype(bf16)


def finish(meta, parts, hands):
    vmem = pl.BlockSpec(memory_space=pltpu.VMEM)
    return pl.pallas_call(
        finish_kernel,
        name="finish",
        in_specs=[pl.BlockSpec(memory_space=pltpu.SMEM)] + [vmem] * 8,
        out_specs=vmem,
        out_shape=jax.ShapeDtypeStruct((4, 32, HD), bf16),
        scratch_shapes=[pltpu.VMEM((4, 64, HD), f32)],
    )(meta, *parts, *hands)


def local(
    new_queries,
    new_keys,
    new_values,
    cached_keys,
    cached_values,
    decode_queries,
    decode_keys,
    decode_values,
    decode_lengths,
    source_block,
):
    ctx = lax.axis_index("ctx")
    tp = lax.axis_index("tp")
    grp = lax.axis_index("grp")
    count = lax.axis_size("ctx")

    def swap(x, bits):
        return lax.ppermute(x, "ctx", [(i, i ^ bits) for i in range(count)])

    pair = jnp.concatenate(
        [cached_keys[:, 0], new_keys[:, 0], cached_values[:, 0], new_values[:, 0]], 0
    )
    pairs = [pair] + [swap(pair, j) for j in (1, 3, 2)]
    pairs = [pairs[0], pairs[1], pairs[3], pairs[2]]

    own_place = 2 * (tp & 1) + grp
    other_place = 2 * (tp & 1) + 1 - grp
    mine = lax.dynamic_index_in_dim(decode_queries, own_place, 1, False)
    theirs = lax.dynamic_index_in_dim(decode_queries, other_place, 1, False)
    got = lax.ppermute(theirs, "grp", [(0, 1), (1, 0)])
    hand_q = jnp.where(grp == (tp >> 1), mine, got).reshape(32, HD)
    source = jnp.broadcast_to(jnp.repeat(source_block.astype(bf16), 8)[:, None], (32, HD))
    query = jnp.concatenate([new_queries[:, 0], jnp.concatenate([hand_q, source], 0)], 1)
    queries = [query] + [swap(query, s << 2) for s in range(1, QS)]

    width = decode_keys.shape[1]
    live = decode_lengths - tp * width
    part = decode_cache(
        live,
        decode_queries.reshape(4, 32, HD),
        decode_keys.reshape(4, width * 4, HD),
        decode_values.reshape(4, width * 4, HD),
    )
    parts = [part] + [
        lax.ppermute(part, "tp", [(i, (i + k) % 4) for i in range(4)]) for k in range(1, 4)
    ]

    slots = [s << 2 for s in range(QS)] + list(range(KS))
    messages = prefill(ctx ^ jnp.array(slots, i32), queries, pairs)
    returned = [messages[0]] + [swap(messages[s], s << 2) for s in range(1, QS)]
    prefill_out, hand = combine(returned)

    def round_of(k):
        pairs_of = []
        for t in range(4):
            for g in range(2):
                to = ((t % 2) * 2 + g + k) % 4
                pairs_of.append((t * 2 + g, to * 2 + t // 2))
        return lax.ppermute(hand, ("tp", "grp"), pairs_of)

    hands = [round_of(k) for k in range(4)]
    places = (tp - jnp.arange(4, dtype=i32)) & 3
    decode_out = finish(places, parts, hands)
    return (prefill_out[:, None, :], decode_out.reshape(4, 4, 8 * HD))


def solution(mesh):
    in_specs = (
        P("ctx", ("tp", "grp"), None),
        P("ctx", ("tp", "grp"), None),
        P("ctx", ("tp", "grp"), None),
        P("ctx", ("tp", "grp"), None),
        P("ctx", ("tp", "grp"), None),
        P("ctx", "grp", None),
        P("ctx", "tp", "grp", None),
        P("ctx", "tp", "grp", None),
        P("ctx"),
        P("ctx"),
    )
    out_specs = (P("ctx", ("tp", "grp"), None), P("ctx", "grp", None))
    return jax.shard_map(local, mesh=mesh, in_specs=in_specs, out_specs=out_specs, check_vma=False)
```

time: 853 us -> 149 us (0.17)
  waiting for transfers between devices: 343 us -> 10.4 us
  blocking collectives: 222 us -> 0 us
  matrix products: 188 us -> 0 us
  Pallas kernels: 0 us -> 68.6 us
  other arithmetic: 72.8 us -> 4.3 us
  starting transfers between devices: 0.16 us -> 55.6 us
  between operations: 14 us -> 0.99 us
    all_gather x4 -> x0, waiting for transfers between devices: 342 us -> none  [the longest x1 173 us: local(): lax.all_gather(cached_values, 'ctx', axis=0, tiled=True)]
    all_gather x5 -> x0, blocking collectives: 222 us -> none  [the longest x1 95.1 us: local(): lax.all_gather(new_keys, 'ctx', axis=0, tiled=True)]
    dot_general x72 -> x0, matrix products: 188 us -> none  [the longest x34 95.7 us: one_block(): jnp.einsum('hrn,nhd->hrd', weights, value_block.astype(jnp.float32), prec...]
    reduce_sum x36 -> x0, other arithmetic: 70.1 us -> none  [the longest x34 69.7 us: one_block(): run_sum = run_sum * factor + jnp.sum(weights, axis=2)]
    pallas_call x0 -> x4, Pallas kernels: none -> 68.6 us  [the longest x1 59.1 us: prefill(): pl.pallas_call(prefill_kernel, name='prefill', in_specs=[pl.BlockSpec(mem...]
    ppermute x0 -> x25, starting transfers between devices: none -> 55.6 us  [the longest x17 34.2 us: swap(): return lax.ppermute(x, 'ctx', [(i, i ^ bits) for i in range(count)])]
    ppermute x0 -> x25, waiting for transfers between devices: none -> 10.4 us  [the longest x17 8.8 us: swap(): return lax.ppermute(x, 'ctx', [(i, i ^ bits) for i in range(count)])]
  transfers between devices with their start and end apart: 4 -> 25, of which waited for: 3 -> 8; matrix products, arithmetic and copies ran while one was open for 1% -> 3% of each run, Pallas kernels for 0% -> 5%
where the time goes in v1:
time: 149 us; the launch traced here: 146 us
  Pallas kernels  68.6 us (46%)
  starting transfers between devices  55.6 us (37%)
  waiting for transfers between devices  10.4 us (7%)
  local copies, waits for them, and re-layouts  6.29 us (4%)
  other arithmetic  4.3 us (3%)
    pallas_call x1, Pallas kernels, prefill(): pl.pallas_call(prefill_kernel, name='prefill', in_specs=[pl.BlockSpec(mem...  59.1 us
    ppermute x17, starting transfers between devices, swap(): return lax.ppermute(x, 'ctx', [(i, i ^ bits) for i in range(count)])  34.2 us
    ppermute x4, starting transfers between devices, round_of(): return lax.ppermute(hand, ('tp', 'grp'), pairs_of)  11.8 us
    ppermute x3, starting transfers between devices, local(): lax.ppermute(part, 'tp', [(i, (i + k) % 4) for i in range(4)])  9.47 us
    ppermute x17, waiting for transfers between devices, swap(): return lax.ppermute(x, 'ctx', [(i, i ^ bits) for i in range(count)])  8.8 us
    pallas_call x1, Pallas kernels, decode_cache(): pl.pallas_call(decode_kernel, name='decode_cache', grid=(rows,), in_specs...  5 us
    unnamed x59, local copies, waits for them, and re-layouts  3.15 us
  transfers between devices with their start and end apart: 25, of which 8 were waited for; matrix products, arithmetic and copies ran while one was open for 3% of the time, Pallas kernels for 5%

profile of v1, /device:TPU:8, one launch (start us, length us, event | category | flops | bytes accessed | tf_op | source)
XLA Modules:
  0.0 146.2 jit_solution(1984171902699666197)
XLA Ops:
  0.7 0.9 constant_dynamic-slice_fusion.1
  1.7 0.7 convert_element_type.3
  2.5 0.3 collective-permute-done
  2.9 0.9 maximum_maximum_fusion.refs_1_
  3.8 1.6 %collective-permute-start.1 = (bf16[64,1152]{1,0:T(8,128)(2,1)S(1)}, bf16[64,1152]{1,0:T(8,128)(2,1)S(1)}, u32[]{:S(2)}, u32[]{:S(2)}) collective-permute-start(bf16[64,1152]{1,0:T(8,128)(2,1)S(1)} %maximum_maximum_fusion.refs_1_), channel_id=1, source_target_pairs={{0,32},{8,40},{16,48},{24,56},{32,0},{40,8},{48,16},{56,24},{64,96... | collective-permute-start | bytes 442376 | tf_op jit(solution)/shard_map/ppermute | solution.py:342
  5.4 1.1 pad_maximum_fusion.refs_9_
  6.5 1.7 %collective-permute-start.10 = (bf16[2176,128]{1,0:T(8,128)(2,1)S(1)}, bf16[2176,128]{1,0:T(8,128)(2,1)S(1)}, u32[]{:S(2)}, u32[]{:S(2)}) collective-permute-start(bf16[2176,128]{1,0:T(8,128)(2,1)S(1)} %pad_maximum_fusion.refs_9_), channel_id=1, source_target_pairs={{0,24},{8,16},{16,8},{24,0},{32,56},{40,48},{48,40},{56,32},{64,88... | collective-permute-start | bytes 1671176 | tf_op jit(solution)/shard_map/ppermute | solution.py:342
  8.2 1.9 %collective-permute-start.8 = (bf16[2176,128]{1,0:T(8,128)(2,1)S(1)}, bf16[2176,128]{1,0:T(8,128)(2,1)S(1)}, u32[]{:S(2)}, u32[]{:S(2)}) collective-permute-start(bf16[2176,128]{1,0:T(8,128)(2,1)S(1)} %pad_maximum_fusion.refs_9_), channel_id=1, source_target_pairs={{0,8},{8,0},{16,24},{24,16},{32,40},{40,32},{48,56},{56,48},{64,72... | collective-permute-start | bytes 1671176 | tf_op jit(solution)/shard_map/ppermute | solution.py:342
  10.1 2.7 %collective-permute-start.2 = (bf16[64,1152]{1,0:T(8,128)(2,1)S(1)}, bf16[64,1152]{1,0:T(8,128)(2,1)S(1)}, u32[]{:S(2)}, u32[]{:S(2)}) collective-permute-start(bf16[64,1152]{1,0:T(8,128)(2,1)S(1)} %maximum_maximum_fusion.refs_1_), channel_id=1, source_target_pairs={{0,64},{8,72},{16,80},{24,88},{32,96},{40,104},{48,112},{56,120},{... | collective-permute-start | bytes 442376 | tf_op jit(solution)/shard_map/ppermute | solution.py:342
  12.8 1.2 collective-permute-start.3
  14.1 2.8 %collective-permute-done.2.refs_3_ = bf16[64,1152]{1,0:T(8,128)(2,1)S(1)} collective-permute-done((bf16[64,1152]{1,0:T(8,128)(2,1)S(1)}, bf16[64,1152]{1,0:T(8,128)(2,1)S(1)}, u32[]{:S(2)}, u32[]{:S(2)}) %collective-permute-start.2) | collective-permute-done | bytes 147488 | tf_op jit(solution)/shard_map/ppermute | solution.py:342
  16.9 1.9 %collective-permute-start.4 = (bf16[64,1152]{1,0:T(8,128)(2,1)S(1)}, bf16[64,1152]{1,0:T(8,128)(2,1)S(1)}, u32[]{:S(2)}, u32[]{:S(2)}) collective-permute-start(bf16[64,1152]{1,0:T(8,128)(2,1)S(1)} %maximum_maximum_fusion.refs_1_), channel_id=1, source_target_pairs={{0,128},{8,136},{16,144},{24,152},{32,160},{40,168},{48,176},{56,1... | collective-permute-start | bytes 442376 | tf_op jit(solution)/shard_map/ppermute | solution.py:342
  18.8 1.1 collective-permute-done.3.refs_4_
  19.9 1.8 %collective-permute-start.5 = (bf16[64,1152]{1,0:T(8,128)(2,1)S(1)}, bf16[64,1152]{1,0:T(8,128)(2,1)S(1)}, u32[]{:S(2)}, u32[]{:S(2)}) collective-permute-start(bf16[64,1152]{1,0:T(8,128)(2,1)S(1)} %maximum_maximum_fusion.refs_1_), channel_id=1, source_target_pairs={{0,160},{8,168},{16,176},{24,184},{32,128},{40,136},{48,144},{56,1... | collective-permute-start | bytes 442376 | tf_op jit(solution)/shard_map/ppermute | solution.py:342
  21.7 0.3 collective-permute-done.4.refs_5_
  22.0 4.0 %collective-permute-start.6 = (bf16[64,1152]{1,0:T(8,128)(2,1)S(1)}, bf16[64,1152]{1,0:T(8,128)(2,1)S(1)}, u32[]{:S(2)}, u32[]{:S(2)}) collective-permute-start(bf16[64,1152]{1,0:T(8,128)(2,1)S(1)} %maximum_maximum_fusion.refs_1_), channel_id=1, source_target_pairs={{0,192},{8,200},{16,208},{24,216},{32,224},{40,232},{48,240},{56,2... | collective-permute-start | bytes 442376 | tf_op jit(solution)/shard_map/ppermute | solution.py:342
  26.0 1.4 collective-permute-done.5.refs_6_
  27.4 3.5 %collective-permute-start.7 = (bf16[64,1152]{1,0:T(8,128)(2,1)S(1)}, bf16[64,1152]{1,0:T(8,128)(2,1)S(1)}, u32[]{:S(2)}, u32[]{:S(2)}) collective-permute-start(bf16[64,1152]{1,0:T(8,128)(2,1)S(1)} %maximum_maximum_fusion.refs_1_), channel_id=1, source_target_pairs={{0,224},{8,232},{16,240},{24,248},{32,192},{40,200},{48,208},{56,2... | collective-permute-start | bytes 442376 | tf_op jit(solution)/shard_map/ppermute | solution.py:342
  30.9 0.5 broadcast_xor_fusion.refs_0_
  31.4 1.3 collective-permute-done.6.refs_7_
  32.7 1.9 %collective-permute-done.7.refs_8_ = bf16[64,1152]{1,0:T(8,128)(2,1)S(1)} collective-permute-done((bf16[64,1152]{1,0:T(8,128)(2,1)S(1)}, bf16[64,1152]{1,0:T(8,128)(2,1)S(1)}, u32[]{:S(2)}, u32[]{:S(2)}) %collective-permute-start.7) | collective-permute-done | bytes 147488 | tf_op jit(solution)/shard_map/ppermute | solution.py:342
  34.8 0.6 copy-done.26
  35.3 0.2 copy-done.17
  35.5 0.2 copy-done.18
  35.8 0.8 copy-done.19
  36.6 59.1 %prefill.1 = (s16[144,512]{1,0:T(8,128)(2,1)}, s16[144,512]{1,0:T(8,128)(2,1)}, s16[144,512]{1,0:T(8,128)(2,1)}, s16[144,512]{1,0:T(8,128)(2,1)}, s16[144,512]{1...) custom-call(s32[12]{0:T(128)} %broadcast_xor_fusion.refs_0_, ...), custom_call_target="tpu_custom_call" | custom-call | flops 27380416512 | bytes 4000000 | tf_op jit(solution)/shard_map/prefill/pallas_call | solution.py:187
  95.8 3.5 %collective-permute-start.12 = (s16[144,512]{1,0:T(8,128)(2,1)}, s16[144,512]{1,0:T(8,128)(2,1)S(1)}, u32[]{:S(2)}, u32[]{:S(2)}) collective-permute-start(s16[144,512]{1,0:T(8,128)(2,1)} %get-tuple-element.14), channel_id=1, source_target_pairs={{0,64},{8,72},{16,80},{24,88},{32,96},{40,104},{48,112},{56,120},{... | collective-permute-start | bytes 442376 | tf_op jit(solution)/shard_map/ppermute | solution.py:342
  99.3 1.1 collective-permute-start.13
  100.4 2.0 %collective-permute-start.14 = (s16[144,512]{1,0:T(8,128)(2,1)}, s16[144,512]{1,0:T(8,128)(2,1)S(1)}, u32[]{:S(2)}, u32[]{:S(2)}) collective-permute-start(s16[144,512]{1,0:T(8,128)(2,1)} %get-tuple-element.16), channel_id=1, source_target_pairs={{0,128},{8,136},{16,144},{24,152},{32,160},{40,168},{48,176},{56,1... | collective-permute-start | bytes 442376 | tf_op jit(solution)/shard_map/ppermute | solution.py:342
  102.4 0.5 broadcast_subtract_fusion.meta
  102.9 0.6 reshape.21.q_ref
  103.6 4.4 %collective-permute-start.16 = (s16[144,512]{1,0:T(8,128)(2,1)}, s16[144,512]{1,0:T(8,128)(2,1)S(1)}, u32[]{:S(2)}, u32[]{:S(2)}) collective-permute-start(s16[144,512]{1,0:T(8,128)(2,1)} %get-tuple-element.18), channel_id=1, source_target_pairs={{0,192},{8,200},{16,208},{24,216},{32,224},{40,232},{48,240},{56,2... | collective-permute-start | bytes 442376 | tf_op jit(solution)/shard_map/ppermute | solution.py:342
  108.0 2.7 %collective-permute-start.17 = (s16[144,512]{1,0:T(8,128)(2,1)}, s16[144,512]{1,0:T(8,128)(2,1)S(1)}, u32[]{:S(2)}, u32[]{:S(2)}) collective-permute-start(s16[144,512]{1,0:T(8,128)(2,1)} %get-tuple-element.19), channel_id=1, source_target_pairs={{0,224},{8,232},{16,240},{24,248},{32,192},{40,200},{48,208},{56,2... | collective-permute-start | bytes 442376 | tf_op jit(solution)/shard_map/ppermute | solution.py:342
  110.6 5.0 %decode_cache.1.refs_1_ = f32[4,64,128]{2,1,0:T(8,128)} custom-call(s32[4]{0:T(128)} %broadcast_subtract_fusion.meta, bf16[4,32,128]{2,1,0:T(8,128)(2,1)} %reshape.21.q_ref, bf16[4,2048,128]{2,1,0:T(8,128)(2,1)} %bitcast.13, bf16[4,2048,128]{2,1,0:T(8,128)(2,1)} %bitcast.14), custom_call_target="tpu_custom_call" | custom-call | flops 200000000 | bytes 4400000 | tf_op jit(solution)/shard_map/decode_cache/pallas_call | solution.py:275
  115.6 3.3 %collective-permute-start.18 = (f32[4,64,128]{2,1,0:T(8,128)}, f32[4,64,128]{2,1,0:T(8,128)S(1)}, u32[]{:S(2)}, u32[]{:S(2)}) collective-permute-start(f32[4,64,128]{2,1,0:T(8,128)} %decode_cache.1.refs_1_), channel_id=1, source_target_pairs={{0,2},{2,4},{4,6},{6,0},{1,3},{3,5},{5,7},{7,1},{8,10},{10,12},{12... | collective-permute-start | bytes 393224 | tf_op jit(solution)/shard_map/ppermute | solution.py:369
  119.0 3.5 %collective-permute-start.19 = (f32[4,64,128]{2,1,0:T(8,128)}, f32[4,64,128]{2,1,0:T(8,128)S(1)}, u32[]{:S(2)}, u32[]{:S(2)}) collective-permute-start(f32[4,64,128]{2,1,0:T(8,128)} %decode_cache.1.refs_1_), channel_id=1, source_target_pairs={{0,4},{2,6},{4,0},{6,2},{1,5},{3,7},{5,1},{7,3},{8,12},{10,14},{12... | collective-permute-start | bytes 393224 | tf_op jit(solution)/shard_map/ppermute | solution.py:369
  122.5 2.7 %collective-permute-start.20 = (f32[4,64,128]{2,1,0:T(8,128)}, f32[4,64,128]{2,1,0:T(8,128)S(1)}, u32[]{:S(2)}, u32[]{:S(2)}) collective-permute-start(f32[4,64,128]{2,1,0:T(8,128)} %decode_cache.1.refs_1_), channel_id=1, source_target_pairs={{0,6},{2,0},{4,2},{6,4},{1,7},{3,1},{5,3},{7,5},{8,14},{10,8},{12,... | collective-permute-start | bytes 393224 | tf_op jit(solution)/shard_map/ppermute | solution.py:369
  125.2 0.6 copy-done.6
  125.8 2.7 %combine.1 = (bf16[64,1024]{1,0:T(8,128)(2,1)}, f32[64,128]{1,0:T(8,128)}) custom-call(s16[144,512]{1,0:T(8,128)(2,1)} %get-tuple-element.12.refs_0_, s16[144,512]{1,0:T(8,128)(2,1)} %copy-done.1, s16[144,512]{1,0:T(8,128)(2,1)} %copy-done.2, s16[144,512]{1,0:T(8,128)(2,1)} %copy-done.3, s16[144,512]{1,0:T(8,128)(2,1)} %copy-done.4, ...), custom_call_target="tpu_custom_call" | custom-call | flops 2000000 | bytes 1300000 | tf_op jit(solution)/shard_map/combine/pallas_call | solution.py:242
  128.6 1.4 collective-permute-start.21
  130.0 4.0 %collective-permute-start.22 = (f32[64,128]{1,0:T(8,128)}, f32[64,128]{1,0:T(8,128)S(1)}, u32[]{:S(2)}, u32[]{:S(2)}) collective-permute-start(f32[64,128]{1,0:T(8,128)} %get-tuple-element.21), channel_id=1, source_target_pairs={{0,2},{1,4},{2,6},{3,0},{4,3},{5,5},{6,7},{7,1},{8,10},{9,12},{10,... | collective-permute-start | bytes 98312 | tf_op jit(solution)/shard_map/ppermute | solution.py:383
  134.0 4.5 %collective-permute-start.23 = (f32[64,128]{1,0:T(8,128)}, f32[64,128]{1,0:T(8,128)S(1)}, u32[]{:S(2)}, u32[]{:S(2)}) collective-permute-start(f32[64,128]{1,0:T(8,128)} %get-tuple-element.21), channel_id=1, source_target_pairs={{0,4},{1,6},{2,0},{3,2},{4,5},{5,7},{6,1},{7,3},{8,12},{9,14},{10,... | collective-permute-start | bytes 98312 | tf_op jit(solution)/shard_map/ppermute | solution.py:383
  138.5 1.9 %collective-permute-start.24 = (f32[64,128]{1,0:T(8,128)}, f32[64,128]{1,0:T(8,128)S(1)}, u32[]{:S(2)}, u32[]{:S(2)}) collective-permute-start(f32[64,128]{1,0:T(8,128)} %get-tuple-element.21), channel_id=1, source_target_pairs={{0,6},{1,0},{2,2},{3,4},{4,7},{5,1},{6,3},{7,5},{8,14},{9,8},{10,1... | collective-permute-start | bytes 98312 | tf_op jit(solution)/shard_map/ppermute | solution.py:383
  140.4 0.6 subtract_and_fusion.refs_0_
  141.1 1.2 collective-permute-done.24.refs_8_
  142.4 0.6 copy-done.16
  143.0 1.8 %finish.1 = bf16[4,32,128]{2,1,0:T(8,128)(2,1)} custom-call(s32[4]{0:T(128)} %subtract_and_fusion.refs_0_, f32[4,64,128]{2,1,0:T(8,128)} %decode_cache.1.refs_1_, f32[4,64,128]{2,1,0:T(8,128)} %copy-done.10, f32[4,64,128]{2,1,0:T(8,128)} %copy-done.11, f32[4,64,128]{2,1,0:T(8,128)} %copy-done.12, f32[64,128]{1,0:T(8,128)} %copy-done.13, ...), custom_call_target="tpu_custom_call" | custom-call | tf_op jit(solution)/shard_map/finish/pallas_call | solution.py:314
  144.8 1.4 reshape.24
  (79 shorter events, 0.7 us)
Async XLA Ops:
  0.6 30.3 %copy-start.28 = (s32[12]{0:T(128)S(1)}, s32[12]{0:T(128)}, u32[]{:S(2)}) copy-start(s32[12]{0:T(128)} %constant.31.clone) | copy-start | bytes 148
  1.5 1.3 collective-permute-start
  3.8 30.9 %copy-start.8 = (bf16[64,1152]{1,0:T(8,128)(2,1)}, bf16[64,1152]{1,0:T(8,128)(2,1)S(1)}, u32[]{:S(2)}) copy-start(bf16[64,1152]{1,0:T(8,128)(2,1)S(1)} %maximum_maximum_fusion.refs_1_) | copy-start | bytes 442372
  3.8 9.0 %collective-permute-start.1 = (bf16[64,1152]{1,0:T(8,128)(2,1)S(1)}, bf16[64,1152]{1,0:T(8,128)(2,1)S(1)}, u32[]{:S(2)}, u32[]{:S(2)}) collective-permute-start(bf16[64,1152]{1,0:T(8,128)(2,1)S(1)} %maximum_maximum_fusion.refs_1_), channel_id=1, source_target_pairs={{0,32},{8,40},{16,48},{24,56},{32,0},{40,8},{48,16},{56,24},{64,96... | collective-permute-start | bytes 442376 | tf_op jit(solution)/shard_map/ppermute | solution.py:342
  6.5 28.2 %copy-start = (bf16[2176,128]{1,0:T(8,128)(2,1)}, bf16[2176,128]{1,0:T(8,128)(2,1)S(1)}, u32[]{:S(2)}) copy-start(bf16[2176,128]{1,0:T(8,128)(2,1)S(1)} %pad_maximum_fusion.refs_9_) | copy-start | bytes 1671172
  6.5 28.1 %collective-permute-start.10 = (bf16[2176,128]{1,0:T(8,128)(2,1)S(1)}, bf16[2176,128]{1,0:T(8,128)(2,1)S(1)}, u32[]{:S(2)}, u32[]{:S(2)}) collective-permute-start(bf16[2176,128]{1,0:T(8,128)(2,1)S(1)} %pad_maximum_fusion.refs_9_), channel_id=1, source_target_pairs={{0,24},{8,16},{16,8},{24,0},{32,56},{40,48},{48,40},{56,32},{64,88... | collective-permute-start | bytes 1671176 | tf_op jit(solution)/shard_map/ppermute | solution.py:342
  8.2 26.5 %collective-permute-start.8 = (bf16[2176,128]{1,0:T(8,128)(2,1)S(1)}, bf16[2176,128]{1,0:T(8,128)(2,1)S(1)}, u32[]{:S(2)}, u32[]{:S(2)}) collective-permute-start(bf16[2176,128]{1,0:T(8,128)(2,1)S(1)} %pad_maximum_fusion.refs_9_), channel_id=1, source_target_pairs={{0,8},{8,0},{16,24},{24,16},{32,40},{40,32},{48,56},{56,48},{64,72... | collective-permute-start | bytes 1671176 | tf_op jit(solution)/shard_map/ppermute | solution.py:342
  10.1 24.6 %collective-permute-start.9 = (bf16[2176,128]{1,0:T(8,128)(2,1)S(1)}, bf16[2176,128]{1,0:T(8,128)(2,1)S(1)}, u32[]{:S(2)}, u32[]{:S(2)}) collective-permute-start(bf16[2176,128]{1,0:T(8,128)(2,1)S(1)} %pad_maximum_fusion.refs_9_), channel_id=1, source_target_pairs={{0,16},{8,24},{16,0},{24,8},{32,48},{40,56},{48,32},{56,40},{64,80... | collective-permute-start | bytes 1671176 | tf_op jit(solution)/shard_map/ppermute | solution.py:342
  10.1 6.8 %collective-permute-start.2 = (bf16[64,1152]{1,0:T(8,128)(2,1)S(1)}, bf16[64,1152]{1,0:T(8,128)(2,1)S(1)}, u32[]{:S(2)}, u32[]{:S(2)}) collective-permute-start(bf16[64,1152]{1,0:T(8,128)(2,1)S(1)} %maximum_maximum_fusion.refs_1_), channel_id=1, source_target_pairs={{0,64},{8,72},{16,80},{24,88},{32,96},{40,104},{48,112},{56,120},{... | collective-permute-start | bytes 442376 | tf_op jit(solution)/shard_map/ppermute | solution.py:342
  12.8 21.9 %copy-start.20 = (bf16[64,1152]{1,0:T(8,128)(2,1)}, bf16[64,1152]{1,0:T(8,128)(2,1)S(1)}, u32[]{:S(2)}) copy-start(bf16[64,1152]{1,0:T(8,128)(2,1)S(1)} %collective-permute-done.1.refs_2_) | copy-start | bytes 442372
  12.8 7.1 %collective-permute-start.3 = (bf16[64,1152]{1,0:T(8,128)(2,1)S(1)}, bf16[64,1152]{1,0:T(8,128)(2,1)S(1)}, u32[]{:S(2)}, u32[]{:S(2)}) collective-permute-start(bf16[64,1152]{1,0:T(8,128)(2,1)S(1)} %maximum_maximum_fusion.refs_1_), channel_id=1, source_target_pairs={{0,96},{8,104},{16,112},{24,120},{32,64},{40,72},{48,80},{56,88},{... | collective-permute-start | bytes 442376 | tf_op jit(solution)/shard_map/ppermute | solution.py:342
  16.9 17.9 %copy-start.21 = (bf16[64,1152]{1,0:T(8,128)(2,1)}, bf16[64,1152]{1,0:T(8,128)(2,1)S(1)}, u32[]{:S(2)}) copy-start(bf16[64,1152]{1,0:T(8,128)(2,1)S(1)} %collective-permute-done.2.refs_3_) | copy-start | bytes 442372
  16.9 5.1 %collective-permute-start.4 = (bf16[64,1152]{1,0:T(8,128)(2,1)S(1)}, bf16[64,1152]{1,0:T(8,128)(2,1)S(1)}, u32[]{:S(2)}, u32[]{:S(2)}) collective-permute-start(bf16[64,1152]{1,0:T(8,128)(2,1)S(1)} %maximum_maximum_fusion.refs_1_), channel_id=1, source_target_pairs={{0,128},{8,136},{16,144},{24,152},{32,160},{40,168},{48,176},{56,1... | collective-permute-start | bytes 442376 | tf_op jit(solution)/shard_map/ppermute | solution.py:342
  19.9 14.8 %copy-start.22 = (bf16[64,1152]{1,0:T(8,128)(2,1)}, bf16[64,1152]{1,0:T(8,128)(2,1)S(1)}, u32[]{:S(2)}) copy-start(bf16[64,1152]{1,0:T(8,128)(2,1)S(1)} %collective-permute-done.3.refs_4_) | copy-start | bytes 442372
  19.9 7.5 %collective-permute-start.5 = (bf16[64,1152]{1,0:T(8,128)(2,1)S(1)}, bf16[64,1152]{1,0:T(8,128)(2,1)S(1)}, u32[]{:S(2)}, u32[]{:S(2)}) collective-permute-start(bf16[64,1152]{1,0:T(8,128)(2,1)S(1)} %maximum_maximum_fusion.refs_1_), channel_id=1, source_target_pairs={{0,160},{8,168},{16,176},{24,184},{32,128},{40,136},{48,144},{56,1... | collective-permute-start | bytes 442376 | tf_op jit(solution)/shard_map/ppermute | solution.py:342
  22.0 12.7 %copy-start.23 = (bf16[64,1152]{1,0:T(8,128)(2,1)}, bf16[64,1152]{1,0:T(8,128)(2,1)S(1)}, u32[]{:S(2)}) copy-start(bf16[64,1152]{1,0:T(8,128)(2,1)S(1)} %collective-permute-done.4.refs_5_) | copy-start | bytes 442372
  22.0 10.7 %collective-permute-start.6 = (bf16[64,1152]{1,0:T(8,128)(2,1)S(1)}, bf16[64,1152]{1,0:T(8,128)(2,1)S(1)}, u32[]{:S(2)}, u32[]{:S(2)}) collective-permute-start(bf16[64,1152]{1,0:T(8,128)(2,1)S(1)} %maximum_maximum_fusion.refs_1_), channel_id=1, source_target_pairs={{0,192},{8,200},{16,208},{24,216},{32,224},{40,232},{48,240},{56,2... | collective-permute-start | bytes 442376 | tf_op jit(solution)/shard_map/ppermute | solution.py:342
  27.4 7.4 %copy-start.24 = (bf16[64,1152]{1,0:T(8,128)(2,1)}, bf16[64,1152]{1,0:T(8,128)(2,1)S(1)}, u32[]{:S(2)}) copy-start(bf16[64,1152]{1,0:T(8,128)(2,1)S(1)} %collective-permute-done.5.refs_6_) | copy-start | bytes 442372
  27.4 7.3 %collective-permute-start.7 = (bf16[64,1152]{1,0:T(8,128)(2,1)S(1)}, bf16[64,1152]{1,0:T(8,128)(2,1)S(1)}, u32[]{:S(2)}, u32[]{:S(2)}) collective-permute-start(bf16[64,1152]{1,0:T(8,128)(2,1)S(1)} %maximum_maximum_fusion.refs_1_), channel_id=1, source_target_pairs={{0,224},{8,232},{16,240},{24,248},{32,192},{40,200},{48,208},{56,2... | collective-permute-start | bytes 442376 | tf_op jit(solution)/shard_map/ppermute | solution.py:342
  31.4 71.0 %copy-start.27 = (s32[4]{0:T(128)S(1)}, s32[4]{0:T(128)}, u32[]{:S(2)}) copy-start(s32[4]{0:T(128)} %param.19) | copy-start | bytes 52
  31.4 71.5 %copy-start.9 = (bf16[4,4,1024]{2,1,0:T(4,128)(2,1)S(1)}, bf16[4,4,1024]{2,1,0:T(4,128)(2,1)}, u32[]{:S(2)}) copy-start(bf16[4,4,1024]{2,1,0:T(4,128)(2,1)} %param.16) | copy-start | bytes 98308
  32.7 2.0 %copy-start.25 = (bf16[64,1152]{1,0:T(8,128)(2,1)}, bf16[64,1152]{1,0:T(8,128)(2,1)S(1)}, u32[]{:S(2)}) copy-start(bf16[64,1152]{1,0:T(8,128)(2,1)S(1)} %collective-permute-done.6.refs_7_) | copy-start | bytes 442372
  34.7 1.1 copy-start.18
  95.6 7.9 %collective-permute-start.11 = (s16[144,512]{1,0:T(8,128)(2,1)}, s16[144,512]{1,0:T(8,128)(2,1)S(1)}, u32[]{:S(2)}, u32[]{:S(2)}) collective-permute-start(s16[144,512]{1,0:T(8,128)(2,1)} %get-tuple-element.13), channel_id=1, source_target_pairs={{0,32},{8,40},{16,48},{24,56},{32,0},{40,8},{48,16},{56,24},{64,96... | collective-permute-start | bytes 442376 | tf_op jit(solution)/shard_map/ppermute | solution.py:342
  95.8 12.2 %collective-permute-start.12 = (s16[144,512]{1,0:T(8,128)(2,1)}, s16[144,512]{1,0:T(8,128)(2,1)S(1)}, u32[]{:S(2)}, u32[]{:S(2)}) collective-permute-start(s16[144,512]{1,0:T(8,128)(2,1)} %get-tuple-element.14), channel_id=1, source_target_pairs={{0,64},{8,72},{16,80},{24,88},{32,96},{40,104},{48,112},{56,120},{... | collective-permute-start | bytes 442376 | tf_op jit(solution)/shard_map/ppermute | solution.py:342
  99.3 16.4 %collective-permute-start.13 = (s16[144,512]{1,0:T(8,128)(2,1)}, s16[144,512]{1,0:T(8,128)(2,1)S(1)}, u32[]{:S(2)}, u32[]{:S(2)}) collective-permute-start(s16[144,512]{1,0:T(8,128)(2,1)} %get-tuple-element.15), channel_id=1, source_target_pairs={{0,96},{8,104},{16,112},{24,120},{32,64},{40,72},{48,80},{56,88},{... | collective-permute-start | bytes 442376 | tf_op jit(solution)/shard_map/ppermute | solution.py:342
  100.4 18.6 %collective-permute-start.14 = (s16[144,512]{1,0:T(8,128)(2,1)}, s16[144,512]{1,0:T(8,128)(2,1)S(1)}, u32[]{:S(2)}, u32[]{:S(2)}) collective-permute-start(s16[144,512]{1,0:T(8,128)(2,1)} %get-tuple-element.16), channel_id=1, source_target_pairs={{0,128},{8,136},{16,144},{24,152},{32,160},{40,168},{48,176},{56,1... | collective-permute-start | bytes 442376 | tf_op jit(solution)/shard_map/ppermute | solution.py:342
  102.4 20.1 %collective-permute-start.15 = (s16[144,512]{1,0:T(8,128)(2,1)}, s16[144,512]{1,0:T(8,128)(2,1)S(1)}, u32[]{:S(2)}, u32[]{:S(2)}) collective-permute-start(s16[144,512]{1,0:T(8,128)(2,1)} %get-tuple-element.17), channel_id=1, source_target_pairs={{0,160},{8,168},{16,176},{24,184},{32,128},{40,136},{48,144},{56,1... | collective-permute-start | bytes 442376 | tf_op jit(solution)/shard_map/ppermute | solution.py:342
  103.5 12.1 %copy-start.1 = (s16[144,512]{1,0:T(8,128)(2,1)}, s16[144,512]{1,0:T(8,128)(2,1)S(1)}, u32[]{:S(2)}) copy-start(s16[144,512]{1,0:T(8,128)(2,1)S(1)} %collective-permute-done.11.refs_1_) | copy-start | bytes 442372
  103.6 21.6 %collective-permute-start.16 = (s16[144,512]{1,0:T(8,128)(2,1)}, s16[144,512]{1,0:T(8,128)(2,1)S(1)}, u32[]{:S(2)}, u32[]{:S(2)}) collective-permute-start(s16[144,512]{1,0:T(8,128)(2,1)} %get-tuple-element.18), channel_id=1, source_target_pairs={{0,192},{8,200},{16,208},{24,216},{32,224},{40,232},{48,240},{56,2... | collective-permute-start | bytes 442376 | tf_op jit(solution)/shard_map/ppermute | solution.py:342
  108.0 7.7 %copy-start.2 = (s16[144,512]{1,0:T(8,128)(2,1)}, s16[144,512]{1,0:T(8,128)(2,1)S(1)}, u32[]{:S(2)}) copy-start(s16[144,512]{1,0:T(8,128)(2,1)S(1)} %collective-permute-done.12.refs_2_) | copy-start | bytes 442372
  108.0 17.2 %collective-permute-start.17 = (s16[144,512]{1,0:T(8,128)(2,1)}, s16[144,512]{1,0:T(8,128)(2,1)S(1)}, u32[]{:S(2)}, u32[]{:S(2)}) collective-permute-start(s16[144,512]{1,0:T(8,128)(2,1)} %get-tuple-element.19), channel_id=1, source_target_pairs={{0,224},{8,232},{16,240},{24,248},{32,192},{40,200},{48,208},{56,2... | collective-permute-start | bytes 442376 | tf_op jit(solution)/shard_map/ppermute | solution.py:342
  115.6 9.5 %copy-start.3 = (s16[144,512]{1,0:T(8,128)(2,1)}, s16[144,512]{1,0:T(8,128)(2,1)S(1)}, u32[]{:S(2)}) copy-start(s16[144,512]{1,0:T(8,128)(2,1)S(1)} %collective-permute-done.13.refs_3_) | copy-start | bytes 442372
  115.6 18.3 %collective-permute-start.18 = (f32[4,64,128]{2,1,0:T(8,128)}, f32[4,64,128]{2,1,0:T(8,128)S(1)}, u32[]{:S(2)}, u32[]{:S(2)}) collective-permute-start(f32[4,64,128]{2,1,0:T(8,128)} %decode_cache.1.refs_1_), channel_id=1, source_target_pairs={{0,2},{2,4},{4,6},{6,0},{1,3},{3,5},{5,7},{7,1},{8,10},{10,12},{12... | collective-permute-start | bytes 393224 | tf_op jit(solution)/shard_map/ppermute | solution.py:369
  119.0 6.2 %copy-start.4 = (s16[144,512]{1,0:T(8,128)(2,1)}, s16[144,512]{1,0:T(8,128)(2,1)S(1)}, u32[]{:S(2)}) copy-start(s16[144,512]{1,0:T(8,128)(2,1)S(1)} %collective-permute-done.14.refs_4_) | copy-start | bytes 442372
  119.0 19.5 %collective-permute-start.19 = (f32[4,64,128]{2,1,0:T(8,128)}, f32[4,64,128]{2,1,0:T(8,128)S(1)}, u32[]{:S(2)}, u32[]{:S(2)}) collective-permute-start(f32[4,64,128]{2,1,0:T(8,128)} %decode_cache.1.refs_1_), channel_id=1, source_target_pairs={{0,4},{2,6},{4,0},{6,2},{1,5},{3,7},{5,1},{7,3},{8,12},{10,14},{12... | collective-permute-start | bytes 393224 | tf_op jit(solution)/shard_map/ppermute | solution.py:369
  122.5 2.7 %copy-start.5 = (s16[144,512]{1,0:T(8,128)(2,1)}, s16[144,512]{1,0:T(8,128)(2,1)S(1)}, u32[]{:S(2)}) copy-start(s16[144,512]{1,0:T(8,128)(2,1)S(1)} %collective-permute-done.15.refs_5_) | copy-start | bytes 442372
  122.5 18.6 %collective-permute-start.20 = (f32[4,64,128]{2,1,0:T(8,128)}, f32[4,64,128]{2,1,0:T(8,128)S(1)}, u32[]{:S(2)}, u32[]{:S(2)}) collective-permute-start(f32[4,64,128]{2,1,0:T(8,128)} %decode_cache.1.refs_1_), channel_id=1, source_target_pairs={{0,6},{2,0},{4,2},{6,4},{1,7},{3,1},{5,3},{7,5},{8,14},{10,8},{12,... | collective-permute-start | bytes 393224 | tf_op jit(solution)/shard_map/ppermute | solution.py:369
  128.6 12.4 %collective-permute-start.21 = (f32[64,128]{1,0:T(8,128)}, f32[64,128]{1,0:T(8,128)S(1)}, u32[]{:S(2)}, u32[]{:S(2)}) collective-permute-start(f32[64,128]{1,0:T(8,128)} %get-tuple-element.21), channel_id=1, source_target_pairs={{0,0},{1,2},{2,4},{3,6},{4,1},{5,3},{6,5},{7,7},{8,8},{9,10},{10,1... | collective-permute-start | bytes 98312 | tf_op jit(solution)/shard_map/ppermute | solution.py:383
  130.0 11.1 %collective-permute-start.22 = (f32[64,128]{1,0:T(8,128)}, f32[64,128]{1,0:T(8,128)S(1)}, u32[]{:S(2)}, u32[]{:S(2)}) collective-permute-start(f32[64,128]{1,0:T(8,128)} %get-tuple-element.21), channel_id=1, source_target_pairs={{0,2},{1,4},{2,6},{3,0},{4,3},{5,5},{6,7},{7,1},{8,10},{9,12},{10,... | collective-permute-start | bytes 98312 | tf_op jit(solution)/shard_map/ppermute | solution.py:383
  134.0 8.3 %copy-start.10 = (f32[4,64,128]{2,1,0:T(8,128)}, f32[4,64,128]{2,1,0:T(8,128)S(1)}, u32[]{:S(2)}) copy-start(f32[4,64,128]{2,1,0:T(8,128)S(1)} %collective-permute-done.18.refs_2_) | copy-start | bytes 393220
  134.0 7.1 %collective-permute-start.23 = (f32[64,128]{1,0:T(8,128)}, f32[64,128]{1,0:T(8,128)S(1)}, u32[]{:S(2)}, u32[]{:S(2)}) collective-permute-start(f32[64,128]{1,0:T(8,128)} %get-tuple-element.21), channel_id=1, source_target_pairs={{0,4},{1,6},{2,0},{3,2},{4,5},{5,7},{6,1},{7,3},{8,12},{9,14},{10,... | collective-permute-start | bytes 98312 | tf_op jit(solution)/shard_map/ppermute | solution.py:383
  138.5 3.8 %copy-start.11 = (f32[4,64,128]{2,1,0:T(8,128)}, f32[4,64,128]{2,1,0:T(8,128)S(1)}, u32[]{:S(2)}) copy-start(f32[4,64,128]{2,1,0:T(8,128)S(1)} %collective-permute-done.19.refs_3_) | copy-start | bytes 393220
  138.5 3.8 %collective-permute-start.24 = (f32[64,128]{1,0:T(8,128)}, f32[64,128]{1,0:T(8,128)S(1)}, u32[]{:S(2)}, u32[]{:S(2)}) collective-permute-start(f32[64,128]{1,0:T(8,128)} %get-tuple-element.21), channel_id=1, source_target_pairs={{0,6},{1,0},{2,2},{3,4},{4,7},{5,1},{6,3},{7,5},{8,14},{9,8},{10,1... | collective-permute-start | bytes 98312 | tf_op jit(solution)/shard_map/ppermute | solution.py:383
  141.0 1.3 copy-start.12
  141.0 1.3 copy-start.13
  141.1 1.3 copy-start.14
  141.1 1.3 copy-start.15
  (6 other events, 4.3 us)

commit v2 on v0

v2 whole, which is shorter than its diff:
```python
import functools
import math

import jax
import jax.numpy as jnp
from jax import lax
from jax.experimental import pallas as pl
from jax.experimental.pallas import tpu as pltpu
from jax.sharding import PartitionSpec as P

f32 = jnp.float32
bf16 = jnp.bfloat16
i16 = jnp.int16
i32 = jnp.int32

HD = 128
GROUPS = 8
TOK = 64
CACHE = 1024
QS = 8
KS = 4
NEWK = KS * TOK
TILE = 4 * TOK
SCALE2 = HD**-0.5 * math.log2(math.e)
NEG = -1e30
NOTHING = -1000.0
CODE = 32767.0
FIRST = 176
SECOND = 144
EARLY = 3
VMEM_LIMIT = 20 * 2**20
VMEM = pl.BlockSpec(memory_space=pltpu.VMEM)
SMEM = pl.BlockSpec(memory_space=pltpu.SMEM)


def contract_last(a, b):
    return lax.dot_general(a, b, (((1,), (1,)), ((), ())), preferred_element_type=f32)


def matmul(a, b):
    return jnp.dot(a, b, preferred_element_type=f32)


def split(p):
    high = p.astype(bf16)
    return high, (p - high.astype(f32)).astype(bf16)


def two_words(x):
    big = jnp.round(x * 32.0)
    return big, jnp.round((x * 32.0 - big) * 32768.0)


def one_number(big, small):
    return (big + small * (1.0 / 32768.0)) * (1.0 / 32.0)


def call(
    kernel, name, outs, count, scratch=(), cost=(1_000_000, 500_000, 1000), vmem=VMEM_LIMIT, **kwargs
):
    return pl.pallas_call(
        kernel,
        name=name,
        out_shape=outs,
        scratch_shapes=scratch,
        compiler_params=pltpu.CompilerParams(vmem_limit_bytes=vmem),
        cost_estimate=pl.CostEstimate(
            flops=cost[0], bytes_accessed=cost[1], transcendentals=cost[2]
        ),
        **kwargs,
    )


def keys_of(pair):
    return pair[0:CACHE, :]


def values_of(pair):
    return pair[CACHE : 2 * CACHE, :].T


def new_of(pairs, which):
    start = 2 * CACHE + which * TOK
    return jnp.concatenate([ref[start : start + TOK, :] for ref in pairs], 0)


def pack_query_kernel(meta, source, new_queries, dec_queries, out, rows):
    upper = meta[0] > 0
    mine, blocks = [], []
    for r in range(4):
        wide = dec_queries[r].astype(f32)
        heads = [
            jnp.concatenate([wide[j : j + 1, g * HD : (g + 1) * HD] for g in range(GROUPS)], 0)
            for j in range(4)
        ]
        rows[r] = jnp.concatenate(heads, 0).astype(bf16)
        mine += [jnp.where(upper, heads[2 + j], heads[j]) for j in range(2)]
        block = jnp.where(meta[1] > 0, source[r], -1).astype(f32)
        blocks.append(jnp.full((16, HD), block, f32).astype(bf16))
    mine = jnp.concatenate(mine, 0).astype(bf16)
    blocks = jnp.concatenate(blocks, 0)
    for s in range(QS):
        out[s, :, 0 : 8 * HD] = new_queries[...]
        out[s, :, 8 * HD : 9 * HD] = mine
        out[s, :, 9 * HD :] = blocks


def tile_queries(queries, b, half):
    start = half * (4 * HD)
    return jnp.concatenate(
        [queries[b, :, start + g * HD : start + (g + 1) * HD] for g in range(4)], 0
    )


def accumulate(tiles, states, blocks):
    work = [(i, t) for i in range(len(blocks)) for t in range(len(tiles))]
    states = list(states)
    following = contract_last(blocks[0][0](), tiles[0])
    for w, (i, t) in enumerate(work):
        scores = following
        if w + 1 < len(work):
            following = contract_last(blocks[work[w + 1][0]][0](), tiles[work[w + 1][1]])
        weights = jnp.exp2(scores * SCALE2)
        if blocks[i][2] is not None:
            weights = jnp.where(blocks[i][2][t], weights, 0.0)
        total, acc = states[t]
        total = total + jnp.sum(weights.reshape(-1, 8, TILE), 0)
        high, low = split(weights)
        values = blocks[i][1]()
        states[t] = (total, acc + matmul(values, high) + matmul(values, low))
    return states


def hand_off(meta, queries, pairs, out):
    rows = QS * 32
    lane = lax.broadcasted_iota(i32, (rows, HD), 1)
    pieces = [(s, r * 16) for s in range(QS) for r in range(4)]
    all_q = [queries[s, :, 8 * HD : 9 * HD].astype(f32) for s in range(QS)]
    all_source = [queries[s, :, 9 * HD :].astype(f32) for s in range(QS)]
    source = jnp.concatenate([all_source[s][a : a + 8] for s, a in pieces], 0)
    keep = jnp.concatenate(
        [
            source == jnp.where(lane < TOK, meta[QS + 2 * j], meta[QS + 2 * j + 1]).astype(f32)
            for j in range(2)
        ],
        1,
    )
    own = meta[QS + KS]
    results = []
    for head in range(2):
        hand_q = jnp.concatenate(
            [all_q[s][a + 8 * head : a + 8 * head + 8] for s, a in pieces], 0
        ).astype(bf16)
        keys = jnp.where(own == head, new_of(pairs, 0), new_of(pairs, 2))
        values = jnp.where(own == head, new_of(pairs, 1), new_of(pairs, 3))
        scores = jnp.where(keep, contract_last(hand_q, keys) * SCALE2, NEG)
        top = jnp.max(scores, 1, keepdims=True)
        weights = jnp.where(keep, jnp.exp2(scores - top), 0.0)
        total = jnp.sum(weights, 1, keepdims=True)
        both = matmul(jnp.concatenate(split(weights), 0), values)
        some = total > 0.0
        safe = jnp.where(some, total, 1.0)
        hand = (both[:rows] + both[rows:]) / safe
        lse = jnp.where(some, jnp.log2(safe) + top, NOTHING)
        most = jnp.maximum(jnp.max(jnp.abs(hand), 1, keepdims=True), 1e-30)
        hand = jnp.round(hand * (CODE / most))
        wide = [jnp.broadcast_to(x, (rows, HD)) for x in (lse, jnp.log2(most))]
        results.append((hand, [[x[:HD].T[0:1], x[HD:].T[0:1]] for x in wide]))
    sums = []
    for s in range(QS):
        slabs = [results[head][0][s * 32 : s * 32 + 32] for head in range(2)]
        out[s, HD + 16 : FIRST, :] = jnp.concatenate(slabs, 1).astype(i32).astype(i16)
        words = []
        for kind in range(2):
            place = s * 32 % HD
            pieces = [results[head][1][kind][s // 4][:, place : place + 32] for head in range(2)]
            row = jnp.concatenate(pieces + [jnp.zeros((1, TILE - 64), f32)], 1)
            words += [*two_words(row)]
        sums.append(words)
    return sums


def prefill_early_kernel(queries, *refs):
    pairs, (acc0, acc1, sum0, sum1, values_t) = refs[:EARLY], refs[EARLY:]
    for j, pair in enumerate(pairs):
        values_t[j] = values_of(pair)
    blocks = [
        (functools.partial(keys_of, pairs[j]), lambda j=j: values_t[j], None) for j in range(EARLY)
    ]

    def step(b, carry):
        tiles = [tile_queries(queries, b, half) for half in range(2)]
        zero = (jnp.zeros((8, TILE), f32), jnp.zeros((HD, TILE), f32))
        states = accumulate(tiles, [zero, zero], blocks)
        (sum0[b], acc0[b]), (sum1[b], acc1[b]) = states
        return carry

    lax.fori_loop(0, QS, step, 0)


def prefill_early(queries, pairs):
    outs = [jax.ShapeDtypeStruct((QS, HD, TILE), f32)] * 2
    outs += [jax.ShapeDtypeStruct((QS, 8, TILE), f32)] * 2
    return call(
        prefill_early_kernel, "prefill_early", outs, 1 + EARLY,
        scratch=[pltpu.VMEM((EARLY, HD, CACHE), bf16)],
        cost=(6 * 4096 * 1024 * EARLY * 128, 4_000_000, 4096 * 1024 * EARLY),
    )(queries, *pairs)


def prefill_late_kernel(half, meta, queries, *refs):
    pairs = refs[:KS]
    acc_in, sum_in, out, out_t, lse_all, values_t = refs[KS:]
    new_keys = new_of(pairs, 0)
    new_values_t = new_of(pairs, 1).T
    for j in range(EARLY, KS):
        values_t[j - EARLY] = values_of(pairs[j])
    cached = [
        (functools.partial(keys_of, pairs[j]), lambda j=j: values_t[j - EARLY], None)
        for j in range(EARLY, KS)
    ]

    def allowed(b):
        offset = lax.broadcasted_iota(i32, (TOK, TILE), 0)
        token = lax.broadcasted_iota(i32, (TOK, TILE), 1) & (TOK - 1)
        limit = token + meta[b] * TOK
        return jnp.concatenate([offset + meta[QS + j] * TOK <= limit for j in range(KS)], 0)

    def step(n, carry):
        places = [4 * n + k for k in range(4)]
        tiles = [tile_queries(queries, b, half) for b in places]
        new = (lambda: new_keys, lambda: new_values_t, [allowed(b) for b in places])
        states = [(sum_in[b], acc_in[b]) for b in places]
        for b, (total, acc) in zip(places, accumulate(tiles, states, cached + [new])):
            total = jnp.sum(total, 0, keepdims=True)
            out_t[b] = acc / total
            lse_all[b] = jnp.log2(total)
        return carry

    lax.fori_loop(0, QS // 4, step, 0)

    lse = lse_all[:, 0, :]
    outside = jnp.where((lse > -60.0) & (lse < 100.0), 0, 1)

    @pl.when(jnp.max(outside) > 0)
    def again():
        blocks = [
            (functools.partial(keys_of, pair), functools.partial(values_of, pair)) for pair in pairs
        ]
        blocks.append((lambda: new_keys, lambda: new_values_t))

        def one(b, carry):
            mask = allowed(b)
            tile = tile_queries(queries, b, half)
            top = jnp.full((1, TILE), NEG, f32)
            total = jnp.zeros((1, TILE), f32)
            acc = jnp.zeros((HD, TILE), f32)
            for i, block in enumerate(blocks):
                scores = contract_last(block[0](), tile) * SCALE2
                if i == KS:
                    scores = jnp.where(mask, scores, NEG)
                new_top = jnp.maximum(top, jnp.max(scores, 0, keepdims=True))
                weights = jnp.exp2(scores - new_top)
                factor = jnp.exp2(top - new_top)
                total = total * factor + jnp.sum(weights, 0, keepdims=True)
                first, second = split(weights)
                values = block[1]()
                acc = acc * factor + matmul(values, first) + matmul(values, second)
                top = new_top
            out_t[b] = acc / total
            lse_all[b] = jnp.log2(total) + top
            return carry

        lax.fori_loop(0, QS, one, 0)

    if half == 0:
        hand_sums = hand_off(meta, queries, pairs, out)
    for s in range(QS):
        result = out_t[s]
        most = jnp.maximum(jnp.max(jnp.abs(result), 0, keepdims=True), 1e-30)
        out[s, 0:HD, :] = jnp.round(result * (CODE / most)).astype(i32).astype(i16)
        words = [*two_words(lse_all[s]), *two_words(jnp.log2(most))]
        words += hand_sums[s] if half == 0 else []
        words += [jnp.zeros((16 - len(words), TILE), f32)]
        out[s, HD : HD + 16, :] = jnp.concatenate(words, 0).astype(i32).astype(i16)


def prefill_late(half, meta, queries, pairs, acc, total):
    return call(
        functools.partial(prefill_late_kernel, half),
        "prefill_second" if half else "prefill_first",
        jax.ShapeDtypeStruct((QS, SECOND if half else FIRST, TILE), i16), 8,
        scratch=[
            pltpu.VMEM((QS, HD, TILE), f32),
            pltpu.VMEM((QS, 1, TILE), f32),
            pltpu.VMEM((KS - EARLY, HD, CACHE), bf16),
        ],
        in_specs=[SMEM] + [VMEM] * 7,
        out_specs=VMEM,
        cost=(6 * 2048 * 1280 * 128, 4_000_000, 2048 * 1280),
    )(meta, queries, *pairs, acc, total)


def merge(outs, lses):
    top = functools.reduce(jnp.maximum, lses)
    factors = [jnp.exp2(x - top) for x in lses]
    total = sum(factors)
    return sum(o * w for o, w in zip(outs, factors)) / total, jnp.log2(total) + top


def combine_kernel(first, second, out):
    for half, parts in enumerate((first, second)):
        tails = [parts[s, HD : HD + 16, :].astype(i32).astype(f32) for s in range(QS)]
        lse = [one_number(tail[0:1], tail[1:2]) for tail in tails]
        most = [one_number(tail[2:3], tail[3:4]) for tail in tails]
        top = functools.reduce(jnp.maximum, lse)
        total = sum(jnp.exp2(x - top) for x in lse) * CODE
        acc = jnp.zeros((HD, TILE), f32)
        for s in range(QS):
            factor = jnp.exp2(lse[s] + most[s] - top) / total
            acc = acc + parts[s, 0:HD, :].astype(i32).astype(f32) * factor
        rows = acc.T
        for g in range(4):
            lanes = slice((half * 4 + g) * HD, (half * 4 + g + 1) * HD)
            out[:, lanes] = rows[g * TOK : (g + 1) * TOK].astype(bf16)


def as_row(wide):
    return wide.T[0:8]


def as_columns(row):
    return jnp.broadcast_to(row[0:1], (HD, HD)).T


def decode_kernel(meta, q_ref, k_ref, v_ref, out_ref, lse_ref):
    row = pl.program_id(0)
    scores = contract_last(q_ref[0], k_ref[0]) * SCALE2
    column = lax.broadcasted_iota(i32, scores.shape, 1)
    head = lax.broadcasted_iota(i32, scores.shape, 0) >> 3
    keep = ((column & 3) == head) & ((column >> 2) < meta[row])
    scores = jnp.where(keep, scores, NEG)
    top = jnp.max(scores, 1, keepdims=True)
    weights = jnp.where(keep, jnp.exp2(scores - top), 0.0)
    total = jnp.sum(weights, 1, keepdims=True)
    both = matmul(jnp.concatenate(split(weights), 0), v_ref[0])
    some = total > 0.0
    safe = jnp.where(some, total, 1.0)
    place = pl.ds(pl.multiple_of(row * 32, 32), 32)
    out_ref[place, :] = (both[0:32] + both[32:64]) / safe
    lse_ref[place, :] = jnp.broadcast_to(jnp.where(some, jnp.log2(safe) + top, NOTHING), (32, HD))

    @pl.when(row == 3)
    def last():
        out_ref[HD:, :] = as_row(lse_ref[...])


def decode_cache(live, queries, keys, values):
    rows, width, unused = keys.shape
    return call(
        decode_kernel, "decode_cache", jax.ShapeDtypeStruct((HD + 8, HD), f32), 4,
        scratch=[pltpu.VMEM((HD, HD), f32)],
        cost=(2_000_000_000, 4_400_000, 262_144),
        grid=(rows,),
        in_specs=[
            SMEM,
            pl.BlockSpec((1, 32, HD), lambda r: (r, 0, 0)),
            pl.BlockSpec((1, width, HD), lambda r: (r, 0, 0)),
            pl.BlockSpec((1, width, HD), lambda r: (r, 0, 0)),
        ],
        out_specs=pl.BlockSpec((HD + 8, HD), lambda r: (0, 0)),
    )(live, queries, keys, values)


def merge_hand_kernel(meta, part, back, out):
    tails = [back[s, HD : HD + 16, :].astype(i32).astype(f32)[4:8, 0:HD] for s in range(QS)]
    columns = jnp.concatenate(tails + [jnp.zeros((HD - 4 * QS, HD), f32)], 0).T
    slabs = [back[s, HD + 16 : FIRST, :].astype(i32).astype(f32) for s in range(QS)]
    heads = []
    for head in range(2):
        outs, sums = [], []
        for s in range(QS):
            four = [
                columns[head * 32 : head * 32 + 32, 4 * s + k : 4 * s + k + 1] for k in range(4)
            ]
            sums.append(one_number(four[0], four[1]))
            scale = jnp.exp2(one_number(four[2], four[3])) / CODE
            outs.append(slabs[s][:, head * HD : (head + 1) * HD] * scale)
        result, lse = merge(outs, sums)
        heads.append((result, jnp.broadcast_to(lse, (32, HD))))
    upper = meta[0] > 0
    blocks, lses = [], []
    for r in range(4):
        for j in range(4):
            fits = upper if j >= 2 else jnp.logical_not(upper)
            result, lse = (x[r * 8 : r * 8 + 8] for x in heads[j % 2])
            blocks.append(jnp.where(fits, result, 0.0))
            lses.append(jnp.where(fits, lse, NOTHING))
    result, lse = merge(
        [part[0:HD], jnp.concatenate(blocks, 0)],
        [as_columns(part[HD:]), jnp.concatenate(lses, 0)],
    )
    most = jnp.maximum(jnp.max(jnp.abs(result), 1, keepdims=True), 1e-30)
    out[0:HD] = jnp.round(result * (CODE / most)).astype(i32).astype(i16)
    wide = jnp.broadcast_to(jnp.log2(most), (HD, HD))
    words = [*two_words(as_row(lse)[0:1]), *two_words(as_row(wide)[0:1]), jnp.zeros((12, HD), f32)]
    out[HD:] = jnp.concatenate(words, 0).astype(i32).astype(i16)


def finish_kernel(meta, *refs):
    parts, (out, placed, rows) = refs[:4], refs[4:]
    for k in range(4):
        placed[meta[2] ^ k] = parts[k][...]
    tails = [placed[t, HD:].astype(i32).astype(f32) for t in range(4)]
    columns = jnp.concatenate(tails + [jnp.zeros((HD - 64, HD), f32)], 0).T
    outs, lses = [], []
    for t in range(4):
        four = [columns[:, 16 * t + k : 16 * t + k + 1] for k in range(4)]
        lses.append(one_number(four[0], four[1]))
        scale = jnp.exp2(one_number(four[2], four[3])) / CODE
        outs.append(placed[t, 0:HD].astype(i32).astype(f32) * scale)
    rows[...] = merge(outs, lses)[0]
    for r in range(4):
        for g in range(GROUPS):
            lanes = slice(g * HD, (g + 1) * HD)
            out[r, :, lanes] = rows[pl.ds(r * 32 + g, 4, stride=8), :].astype(bf16)


def local(
    new_queries,
    new_keys,
    new_values,
    cached_keys,
    cached_values,
    decode_queries,
    decode_keys,
    decode_values,
    decode_lengths,
    source_block,
):
    ctx = lax.axis_index("ctx")
    tp = lax.axis_index("tp")
    grp = lax.axis_index("grp")
    count = lax.axis_size("ctx")
    struct = jax.ShapeDtypeStruct

    def exchange(x):
        groups = [
            [z + 4 * (k >> 1) + y + (k & 1) for k in range(QS)] for z in (0, 16) for y in (0, 2)
        ]
        return lax.all_to_all(x, "ctx", 0, 0, axis_index_groups=groups, tiled=True)

    def other_core(x):
        return lax.ppermute(x, "grp", [(0, 1), (1, 0)])

    own_new = (new_keys[:, 0], new_values[:, 0])
    pair = jnp.concatenate(
        [cached_keys[:, 0], cached_values[:, 0], *own_new, *[other_core(x) for x in own_new]], 0
    )

    def swap(x, bits):
        return lax.ppermute(x, "ctx", [(i, i ^ bits) for i in range(count)])

    sent = [swap(pair, 16), swap(pair, 3)]

    holds = (grp == (tp >> 1)).astype(i32)
    flags = jnp.stack([tp & 1, holds, tp]).astype(i32)
    query, dec_queries = call(
        pack_query_kernel, "pack_query",
        [struct((QS, TOK, 10 * HD), bf16), struct((4, 32, HD), bf16)], 4,
        in_specs=[SMEM] * 2 + [VMEM] * 2, out_specs=[VMEM] * 2, vmem=56 * 2**20,
    )(flags, source_block, new_queries[:, 0], decode_queries)
    queries = exchange(query)

    width = decode_keys.shape[1]
    live = decode_lengths - tp * width
    part = decode_cache(
        live,
        dec_queries,
        decode_keys.reshape(4, width * 4, HD),
        decode_values.reshape(4, width * 4, HD),
    )

    queries, part = lax.optimization_barrier((queries, part))
    blocks = [(ctx & 18) + 4 * (k >> 1) + (k & 1) for k in range(QS)]
    blocks += [ctx ^ bits for bits in (0, 16, 3, 19)]
    meta = jnp.stack(blocks + [grp]).astype(i32)
    later, *sent = lax.optimization_barrier((pair, *sent))
    everyone = [pair, *sent, swap(later, 19)]
    acc0, acc1, sum0, sum1 = prefill_early(queries, everyone[:EARLY])
    first = prefill_late(0, meta, queries, everyone, acc0, sum0)
    meta, first = lax.optimization_barrier((meta, first))
    first_back = exchange(first)
    second = prefill_late(1, meta, queries, everyone, acc1, sum1)
    second_back = exchange(second)

    hand_back, second = lax.optimization_barrier((first_back, second))
    part = call(
        merge_hand_kernel, "merge_hand", struct((HD + 16, HD), i16), 3,
        in_specs=[SMEM] + [VMEM] * 2, out_specs=VMEM,
    )(flags, part, hand_back)
    parts = [part] + [lax.ppermute(part, "tp", [(i, i ^ k) for i in range(4)]) for k in (1, 2, 3)]
    out = call(
        combine_kernel, "combine", struct((TOK, 8 * HD), bf16), 2,
        cost=(2_000_000_000, 1_300_000, 10_000),
    )(first_back, second_back)
    decode_out = call(
        finish_kernel, "finish", struct((4, 4, 8 * HD), bf16), 5,
        scratch=[pltpu.VMEM((4, HD + 16, HD), i16), pltpu.VMEM((HD, HD), f32)],
        in_specs=[SMEM] + [VMEM] * 4, out_specs=VMEM,
    )(flags, *parts)
    return (out[:, None, :], decode_out)


def solution(mesh):
    in_specs = (
        P("ctx", ("tp", "grp"), None),
        P("ctx", ("tp", "grp"), None),
        P("ctx", ("tp", "grp"), None),
        P("ctx", ("tp", "grp"), None),
        P("ctx", ("tp", "grp"), None),
        P("ctx", "grp", None),
        P("ctx", "tp", "grp", None),
        P("ctx", "tp", "grp", None),
        P("ctx"),
        P("ctx"),
    )
    out_specs = (P("ctx", ("tp", "grp"), None), P("ctx", "grp", None))
    return jax.shard_map(local, mesh=mesh, in_specs=in_specs, out_specs=out_specs, check_vma=False)
```

time: 853 us -> 129 us (0.15)
  waiting for transfers between devices: 343 us -> 12.2 us
  blocking collectives: 222 us -> 0 us
  matrix products: 188 us -> 0 us
  Pallas kernels: 0 us -> 76.6 us
  other arithmetic: 72.8 us -> 0.67 us
  starting transfers between devices: 0.16 us -> 31 us
  between operations: 14 us -> 0.81 us
    all_gather x4 -> x0, waiting for transfers between devices: 342 us -> none  [the longest x1 173 us: local(): lax.all_gather(cached_values, 'ctx', axis=0, tiled=True)]
    all_gather x5 -> x0, blocking collectives: 222 us -> none  [the longest x1 95.1 us: local(): lax.all_gather(new_keys, 'ctx', axis=0, tiled=True)]
    dot_general x72 -> x0, matrix products: 188 us -> none  [the longest x34 95.7 us: one_block(): jnp.einsum('hrn,nhd->hrd', weights, value_block.astype(jnp.float32), prec...]
    pallas_call x0 -> x8, Pallas kernels: none -> 76.6 us  [the longest x2 50 us: prefill_late(): call(functools.partial(prefill_late_kernel, half), 'prefill_second' if ha...]
    reduce_sum x36 -> x0, other arithmetic: 70.1 us -> none  [the longest x34 69.7 us: one_block(): run_sum = run_sum * factor + jnp.sum(weights, axis=2)]
    all_to_all x0 -> x3, starting transfers between devices: none -> 17.5 us  [exchange(): return lax.all_to_all(x, 'ctx', 0, 0, axis_index_groups=groups, tiled=True)]
    ppermute x0 -> x8, starting transfers between devices: none -> 13.4 us  [the longest x3 7.92 us: local(): lax.ppermute(part, 'tp', [(i, i ^ k) for i in range(4)])]
    ppermute x0 -> x8, waiting for transfers between devices: none -> 11 us  [the longest x3 6.67 us: swap(): return lax.ppermute(x, 'ctx', [(i, i ^ bits) for i in range(count)])]
  transfers between devices with their start and end apart: 4 -> 11, of which waited for: 3 -> 4; matrix products, arithmetic and copies ran while one was open for 1% -> 1% of each run, Pallas kernels for 0% -> 39%
where the time goes in v2:
time: 129 us; the launch traced here: 128 us
  Pallas kernels  76.6 us (59%)
  starting transfers between devices  31 us (24%)
  waiting for transfers between devices  12.2 us (9%)
  local copies, waits for them, and re-layouts  6.68 us (5%)
    pallas_call x2, Pallas kernels, prefill_late(): call(functools.partial(prefill_late_kernel, half), 'prefill_second' if ha...  50 us
    all_to_all x3, starting transfers between devices, exchange(): return lax.all_to_all(x, 'ctx', 0, 0, axis_index_groups=groups, tiled=True)  17.5 us
    pallas_call x1, Pallas kernels, prefill_early(): call(prefill_early_kernel, 'prefill_early', outs, 1 + EARLY, scratch=[plt...  17.1 us
    ppermute x3, starting transfers between devices, local(): lax.ppermute(part, 'tp', [(i, i ^ k) for i in range(4)])  7.92 us
    ppermute x3, waiting for transfers between devices, swap(): return lax.ppermute(x, 'ctx', [(i, i ^ bits) for i in range(count)])  6.67 us
    unnamed x31, local copies, waits for them, and re-layouts  6.58 us
    ppermute x3, starting transfers between devices, swap(): return lax.ppermute(x, 'ctx', [(i, i ^ bits) for i in range(count)])  4.93 us
    ppermute x3, waiting for transfers between devices, local(): lax.ppermute(part, 'tp', [(i, i ^ k) for i in range(4)])  4.33 us
  transfers between devices with their start and end apart: 11, of which 4 were waited for; matrix products, arithmetic and copies ran while one was open for 1% of the time, Pallas kernels for 39%

profile of v2, /device:TPU:8, one launch (start us, length us, event | category | flops | bytes accessed | tf_op | source)
XLA Modules:
  0.0 128.0 jit_solution(8192716116847032614)
XLA Ops:
  0.6 0.0 copy-start.11
  0.6 0.0 copy-start.10
  0.7 0.0 copy-start.8
  0.7 0.0 copy-start.9
  0.7 0.0 copy-start.12
  0.7 0.1 collective-permute-start.1
  0.8 0.5 collective-permute-start
  1.3 0.7 pad_add_fusion.meta
  1.9 2.1 %pack_query.1 = (bf16[8,64,1280]{2,1,0:T(8,128)(2,1)}, bf16[4,32,128]{2,1,0:T(8,128)(2,1)}) custom-call(s32[3]{0:T(128)} %pad_add_fusion.meta, s32[4]{0:T(128)} %source.1, bf16[64,1024]{1,0:T(8,128)(2,1)} %bitcast.30, bf16[4,4,1024]{2,1,0:T(4,128)(2,1)} %dec_queries.1), custom_call_target="tpu_custom_call" | custom-call | flops 1000000 | bytes 500000 | tf_op jit(solution)/shard_map/pack_query/pallas_call | solution.py:468
  4.1 5.9 %all-to-all-start = ((bf16[8,64,1280]{2,1,0:T(8,128)(2,1)}), bf16[8,64,1280]{2,1,0:T(8,128)(2,1)S(1)}, u32[]{:S(2)}, u32[]{:S(2)}) async-start(bf16[8,64,1280]{2,1,0:T(8,128)(2,1)} %get-tuple-element.16), calls=%async_computation | async-start | bytes 2621440 | tf_op jit(solution)/shard_map/all_to_all | solution.py:451
  10.0 0.0 copy-done.8
  10.0 0.0 copy-done.9
  10.0 0.0 copy-done.10
  10.1 0.0 copy-done.11
  10.1 0.0 collective-permute-done
  10.1 0.0 collective-permute-done.1
  10.1 0.9 collective-permute-start.3
  11.1 1.9 %collective-permute-start.2 = (bf16[2304,128]{1,0:T(8,128)(2,1)S(1)}, bf16[2304,128]{1,0:T(8,128)(2,1)S(1)}, u32[]{:S(2)}, u32[]{:S(2)}) collective-permute-start(bf16[2304,128]{1,0:T(8,128)(2,1)S(1)} %constant_dynamic-update-slice_fusion.refs_0_), channel_id=1, source_target_pairs={{0,128},{8,136},{16,144},{24,152},{32,160},{40,168},{48,176},{56,1... | collective-permute-start | bytes 1769480 | tf_op jit(solution)/shard_map/ppermute | solution.py:462
  13.0 0.1 stack.70.meta
  13.1 0.0 copy-done.5
  13.1 0.0 copy-start.1
  13.1 1.6 %copy-done.1 = bf16[4,512,4,128]{3,2,1,0:T(4,128)(2,1)S(1)} copy-done((bf16[4,512,4,128]{3,2,1,0:T(4,128)(2,1)S(1)}, bf16[4,512,4,128]{3,2,1,0:T(4,128)(2,1)}, u32[]{:S(2)}) %copy-start.1) | copy-done | bytes 2097176
  14.7 1.6 %copy-done.2 = bf16[4,512,4,128]{3,2,1,0:T(4,128)(2,1)S(1)} copy-done((bf16[4,512,4,128]{3,2,1,0:T(4,128)(2,1)S(1)}, bf16[4,512,4,128]{3,2,1,0:T(4,128)(2,1)}, u32[]{:S(2)}) %copy-start.2) | copy-done | bytes 2097176
  16.3 3.1 %decode_cache.1.part = f32[136,128]{1,0:T(8,128)S(1)} custom-call(s32[4]{0:T(128)S(1)} %broadcast_subtract_fusion.meta, bf16[4,32,128]{2,1,0:T(8,128)(2,1)S(1)} %copy-done.5, bf16[4,2048,128]{2,1,0:T(8,128)(2,1)S(1)} %bitcast.28, bf16[4,2048,128]{2,1,0:T(8,128)(2,1)S(1)} %bitcast.29), custom_call_target="tpu_custom_call" | custom-call | flops 2000000000 | bytes 4400000 | tf_op jit(solution)/shard_map/decode_cache/pallas_call | solution.py:360
  19.3 5.8 %collective-permute-done.3.refs_2_ = bf16[2304,128]{1,0:T(8,128)(2,1)S(1)} collective-permute-done((bf16[2304,128]{1,0:T(8,128)(2,1)S(1)}, bf16[2304,128]{1,0:T(8,128)(2,1)S(1)}, u32[]{:S(2)}, u32[]{:S(2)}) %collective-permute-start.3) | collective-permute-done | bytes 589856 | tf_op jit(solution)/shard_map/ppermute | solution.py:462
  25.2 0.8 collective-permute-done.2.refs_1_
  26.0 2.1 %collective-permute-start.4 = (bf16[2304,128]{1,0:T(8,128)(2,1)S(1)}, bf16[2304,128]{1,0:T(8,128)(2,1)}, u32[]{:S(2)}, u32[]{:S(2)}) collective-permute-start(bf16[2304,128]{1,0:T(8,128)(2,1)S(1)} %constant_dynamic-update-slice_fusion.refs_0_), channel_id=1, source_target_pairs={{0,152},{8,144},{16,136},{24,128},{32,184},{40,176},{48,168},{56,1... | collective-permute-start | bytes 1769480 | tf_op jit(solution)/shard_map/ppermute | solution.py:462
  28.1 1.2 all-to-all-done.queries
  29.3 17.1 %prefill_early.1 = (f32[8,128,256]{2,1,0:T(8,128)S(1)}, f32[8,128,256]{2,1,0:T(8,128)S(1)}, f32[8,8,256]{2,1,0:T(8,128)S(1)}, f32[8,8,256]{2,1,0:T(8,128)S(1)}) custom-call(bf16[8,64,1280]{2,1,0:T(8,128)(2,1)S(1)} %all-to-all-done.queries, bf16[2304,128]{1,0:T(8,128)(2,1)S(1)} %constant_dynamic-update-slice_fusion.refs_0_, ...), custom_call_target="tpu_custom_call" | custom-call | flops 9663676416 | bytes 4000000 | tf_op jit(solution)/shard_map/prefill_early/pallas_call | solution.py:204
  46.4 1.0 copy-done.6
  47.4 0.0 collective-permute-done.4.refs_3_
  47.4 25.3 %prefill_first.1 = s16[8,176,256]{2,1,0:T(8,128)(2,1)} custom-call(s32[13]{0:T(128)S(1)} %stack.70.meta, bf16[8,64,1280]{2,1,0:T(8,128)(2,1)S(1)} %all-to-all-done.queries, bf16[2304,128]{1,0:T(8,128)(2,1)S(1)} %constant_dynamic-update-slice_fusion.refs_0_, bf16[2304,128]{1,0:T(8,128)(2,1)S(1)} %collective-permute-done.2.refs_1_, ...), custom_call_target="tpu_custom_call" | custom-call | flops 2013265920 | bytes 4000000 | tf_op jit(solution)/shard_map/prefill_first/pallas_call | solution.py:289
  72.8 5.9 %all-to-all-start.1 = ((s16[8,176,256]{2,1,0:T(8,128)(2,1)}), s16[8,176,256]{2,1,0:T(8,128)(2,1)S(1)}, u32[]{:S(2)}, u32[]{:S(2)}) async-start(s16[8,176,256]{2,1,0:T(8,128)(2,1)} %prefill_first.1), calls=%async_computation.1 | async-start | bytes 1441792 | tf_op jit(solution)/shard_map/all_to_all | solution.py:451
  78.7 1.1 copy-done.4
  79.8 1.2 copy-done.7
  81.0 24.7 %prefill_second.1 = s16[8,144,256]{2,1,0:T(8,128)(2,1)} custom-call(s32[13]{0:T(128)S(1)} %stack.70.meta, bf16[8,64,1280]{2,1,0:T(8,128)(2,1)S(1)} %all-to-all-done.queries, bf16[2304,128]{1,0:T(8,128)(2,1)S(1)} %constant_dynamic-update-slice_fusion.refs_0_, bf16[2304,128]{1,0:T(8,128)(2,1)S(1)} %copy-done.4, ...), custom_call_target="tpu_custom_call" | custom-call | flops 2013265920 | bytes 4000000 | tf_op jit(solution)/shard_map/prefill_second/pallas_call | solution.py:289
  105.6 0.0 all-to-all-done.1.first.back
  105.7 5.7 %all-to-all-start.2 = ((s16[8,144,256]{2,1,0:T(8,128)(2,1)}), s16[8,144,256]{2,1,0:T(8,128)(2,1)S(1)}, u32[]{:S(2)}, u32[]{:S(2)}) async-start(s16[8,144,256]{2,1,0:T(8,128)(2,1)} %prefill_second.1), calls=%async_computation.2 | async-start | bytes 1179648 | tf_op jit(solution)/shard_map/all_to_all | solution.py:451
  111.4 1.5 %merge_hand.1.refs_0_ = s16[144,128]{1,0:T(8,128)(2,1)S(1)} custom-call(s32[3]{0:T(128)S(1)} %copy-done, f32[136,128]{1,0:T(8,128)S(1)} %decode_cache.1.part, s16[8,176,256]{2,1,0:T(8,128)(2,1)S(1)} %all-to-all-done.1.first.back), custom_call_target="tpu_custom_call" | custom-call | flops 1000000 | bytes 500000 | tf_op jit(solution)/shard_map/merge_hand/pallas_call | solution.py:498
  112.8 5.5 %collective-permute-start.7 = (s16[144,128]{1,0:T(8,128)(2,1)S(1)}, s16[144,128]{1,0:T(8,128)(2,1)S(1)}, u32[]{:S(2)}, u32[]{:S(2)}) collective-permute-start(s16[144,128]{1,0:T(8,128)(2,1)S(1)} %merge_hand.1.refs_0_), channel_id=1, source_target_pairs={{0,6},{2,4},{4,2},{6,0},{1,7},{3,5},{5,3},{7,1},{8,14},{10,12},{12... | collective-permute-start | bytes 110600 | tf_op jit(solution)/shard_map/ppermute | solution.py:502
  118.3 1.4 %collective-permute-start.6 = (s16[144,128]{1,0:T(8,128)(2,1)S(1)}, s16[144,128]{1,0:T(8,128)(2,1)S(1)}, u32[]{:S(2)}, u32[]{:S(2)}) collective-permute-start(s16[144,128]{1,0:T(8,128)(2,1)S(1)} %merge_hand.1.refs_0_), channel_id=1, source_target_pairs={{0,4},{2,6},{4,0},{6,2},{1,5},{3,7},{5,1},{7,3},{8,12},{10,14},{12... | collective-permute-start | bytes 110600 | tf_op jit(solution)/shard_map/ppermute | solution.py:502
  119.7 1.0 collective-permute-start.5
  120.8 0.0 all-to-all-done.2.second
  120.8 1.1 combine.1
  121.8 0.0 collective-permute-done.7.refs_3_
  121.8 4.3 %collective-permute-done.6.refs_2_ = s16[144,128]{1,0:T(8,128)(2,1)S(1)} collective-permute-done((s16[144,128]{1,0:T(8,128)(2,1)S(1)}, s16[144,128]{1,0:T(8,128)(2,1)S(1)}, u32[]{:S(2)}, u32[]{:S(2)}) %collective-permute-start.6) | collective-permute-done | bytes 36896 | tf_op jit(solution)/shard_map/ppermute | solution.py:502
  126.2 0.0 collective-permute-done.5.refs_1_
  126.2 1.8 %finish.1 = bf16[4,4,1024]{2,1,0:T(4,128)(2,1)} custom-call(s32[3]{0:T(128)S(1)} %copy-done, s16[144,128]{1,0:T(8,128)(2,1)S(1)} %merge_hand.1.refs_0_, s16[144,128]{1,0:T(8,128)(2,1)S(1)} %collective-permute-done.5.refs_1_, s16[144,128]{1,0:T(8,128)(2,1)S(1)} %collective-permute-done.6.refs_2_, s16[144,128]{1,0:T(8,128)(2,1)S(1)} %collective-permute-done.7.refs_3_), custom_call_target="tpu_custom_call" | custom-call | flops 1000000 | bytes 500000 | tf_op jit(solution)/shard_map/finish/pallas_call | solution.py:507
  (17 shorter events, 0.1 us)
Async XLA Ops:
  0.6 9.4 %copy-start.11 = (bf16[64,1,128]{2,0,1:T(8,128)(2,1)S(1)}, bf16[64,1,128]{2,0,1:T(8,128)(2,1)}, u32[]{:S(2)}) copy-start(bf16[64,1,128]{2,0,1:T(8,128)(2,1)} %param.12) | copy-start | bytes 49156
  0.6 9.4 %copy-start.10 = (bf16[64,1,128]{2,0,1:T(8,128)(2,1)S(1)}, bf16[64,1,128]{2,0,1:T(8,128)(2,1)}, u32[]{:S(2)}) copy-start(bf16[64,1,128]{2,0,1:T(8,128)(2,1)} %param.11) | copy-start | bytes 49156
  0.7 9.3 %copy-start.8 = (bf16[1024,1,128]{2,0,1:T(8,128)(2,1)S(1)}, bf16[1024,1,128]{2,0,1:T(8,128)(2,1)}, u32[]{:S(2)}) copy-start(bf16[1024,1,128]{2,0,1:T(8,128)(2,1)} %param.13) | copy-start | bytes 786436
  0.7 9.3 %copy-start.9 = (bf16[1024,1,128]{2,0,1:T(8,128)(2,1)S(1)}, bf16[1024,1,128]{2,0,1:T(8,128)(2,1)}, u32[]{:S(2)}) copy-start(bf16[1024,1,128]{2,0,1:T(8,128)(2,1)} %param.14) | copy-start | bytes 786436
  0.7 12.4 %copy-start.12 = (s32[4]{0:T(128)S(1)}, s32[4]{0:T(128)}, u32[]{:S(2)}) copy-start(s32[4]{0:T(128)} %param.18) | copy-start | bytes 52
  0.7 9.4 %collective-permute-start.1 = (bf16[64,128]{1,0:T(8,128)(2,1)}, bf16[64,128]{1,0:T(8,128)(2,1)S(1)}, u32[]{:S(2)}, u32[]{:S(2)}) collective-permute-start(bf16[64,128]{1,0:T(8,128)(2,1)} %bitcast.32), channel_id=1, source_target_pairs={{0,1},{1,0},{2,3},{3,2},{4,5},{5,4},{6,7},{7,6},{8,9},{9,8},{10,11... | collective-permute-start | bytes 49160 | tf_op jit(solution)/shard_map/ppermute | solution.py:454
  0.8 9.3 %collective-permute-start = (bf16[64,128]{1,0:T(8,128)(2,1)}, bf16[64,128]{1,0:T(8,128)(2,1)S(1)}, u32[]{:S(2)}, u32[]{:S(2)}) collective-permute-start(bf16[64,128]{1,0:T(8,128)(2,1)} %bitcast.31), channel_id=1, source_target_pairs={{0,1},{1,0},{2,3},{3,2},{4,5},{5,4},{6,7},{7,6},{8,9},{9,8},{10,11... | collective-permute-start | bytes 49160 | tf_op jit(solution)/shard_map/ppermute | solution.py:454
  4.1 9.0 %copy-start.5 = (bf16[4,32,128]{2,1,0:T(8,128)(2,1)S(1)}, bf16[4,32,128]{2,1,0:T(8,128)(2,1)}, u32[]{:S(2)}) copy-start(bf16[4,32,128]{2,1,0:T(8,128)(2,1)} %get-tuple-element.17.q_ref) | copy-start | bytes 98308
  4.1 25.3 %all-to-all-start = ((bf16[8,64,1280]{2,1,0:T(8,128)(2,1)}), bf16[8,64,1280]{2,1,0:T(8,128)(2,1)S(1)}, u32[]{:S(2)}, u32[]{:S(2)}) async-start(bf16[8,64,1280]{2,1,0:T(8,128)(2,1)} %get-tuple-element.16), calls=%async_computation | async-start | bytes 2621440 | tf_op jit(solution)/shard_map/all_to_all | solution.py:451
  10.1 15.0 %collective-permute-start.3 = (bf16[2304,128]{1,0:T(8,128)(2,1)S(1)}, bf16[2304,128]{1,0:T(8,128)(2,1)S(1)}, u32[]{:S(2)}, u32[]{:S(2)}) collective-permute-start(bf16[2304,128]{1,0:T(8,128)(2,1)S(1)} %constant_dynamic-update-slice_fusion.refs_0_), channel_id=1, source_target_pairs={{0,24},{8,16},{16,8},{24,0},{32,56},{40,48},{48,40},{56,32},{64,88... | collective-permute-start | bytes 1769480 | tf_op jit(solution)/shard_map/ppermute | solution.py:462
  11.1 14.9 %collective-permute-start.2 = (bf16[2304,128]{1,0:T(8,128)(2,1)S(1)}, bf16[2304,128]{1,0:T(8,128)(2,1)S(1)}, u32[]{:S(2)}, u32[]{:S(2)}) collective-permute-start(bf16[2304,128]{1,0:T(8,128)(2,1)S(1)} %constant_dynamic-update-slice_fusion.refs_0_), channel_id=1, source_target_pairs={{0,128},{8,136},{16,144},{24,152},{32,160},{40,168},{48,176},{56,1... | collective-permute-start | bytes 1769480 | tf_op jit(solution)/shard_map/ppermute | solution.py:462
  13.1 1.6 %copy-start.1 = (bf16[4,512,4,128]{3,2,1,0:T(4,128)(2,1)S(1)}, bf16[4,512,4,128]{3,2,1,0:T(4,128)(2,1)}, u32[]{:S(2)}) copy-start(bf16[4,512,4,128]{3,2,1,0:T(4,128)(2,1)} %param.16) | copy-start | bytes 6291460
  14.7 1.6 %copy-start.2 = (bf16[4,512,4,128]{3,2,1,0:T(4,128)(2,1)S(1)}, bf16[4,512,4,128]{3,2,1,0:T(4,128)(2,1)}, u32[]{:S(2)}) copy-start(bf16[4,512,4,128]{3,2,1,0:T(4,128)(2,1)} %param.17) | copy-start | bytes 6291460
  26.0 21.4 %copy-start.3 = (bf16[2304,128]{1,0:T(8,128)(2,1)}, bf16[2304,128]{1,0:T(8,128)(2,1)S(1)}, u32[]{:S(2)}) copy-start(bf16[2304,128]{1,0:T(8,128)(2,1)S(1)} %collective-permute-done.2.refs_1_) | copy-start | bytes 1769476
  26.0 21.4 %collective-permute-start.4 = (bf16[2304,128]{1,0:T(8,128)(2,1)S(1)}, bf16[2304,128]{1,0:T(8,128)(2,1)}, u32[]{:S(2)}, u32[]{:S(2)}) collective-permute-start(bf16[2304,128]{1,0:T(8,128)(2,1)S(1)} %constant_dynamic-update-slice_fusion.refs_0_), channel_id=1, source_target_pairs={{0,152},{8,144},{16,136},{24,128},{32,184},{40,176},{48,168},{56,1... | collective-permute-start | bytes 1769480 | tf_op jit(solution)/shard_map/ppermute | solution.py:462
  46.4 1.0 copy-start.6
  72.8 32.9 %all-to-all-start.1 = ((s16[8,176,256]{2,1,0:T(8,128)(2,1)}), s16[8,176,256]{2,1,0:T(8,128)(2,1)S(1)}, u32[]{:S(2)}, u32[]{:S(2)}) async-start(s16[8,176,256]{2,1,0:T(8,128)(2,1)} %prefill_first.1), calls=%async_computation.1 | async-start | bytes 1441792 | tf_op jit(solution)/shard_map/all_to_all | solution.py:451
  78.7 1.1 copy-start.4
  79.8 1.2 copy-start.7
  81.0 30.4 %copy-start = (s32[3]{0:T(128)S(1)}, s32[3]{0:T(128)}, u32[]{:S(2)}) copy-start(s32[3]{0:T(128)} %pad_add_fusion.meta) | copy-start | bytes 40
  105.7 15.1 %all-to-all-start.2 = ((s16[8,144,256]{2,1,0:T(8,128)(2,1)}), s16[8,144,256]{2,1,0:T(8,128)(2,1)S(1)}, u32[]{:S(2)}, u32[]{:S(2)}) async-start(s16[8,144,256]{2,1,0:T(8,128)(2,1)} %prefill_second.1), calls=%async_computation.2 | async-start | bytes 1179648 | tf_op jit(solution)/shard_map/all_to_all | solution.py:451
  112.8 9.0 %collective-permute-start.7 = (s16[144,128]{1,0:T(8,128)(2,1)S(1)}, s16[144,128]{1,0:T(8,128)(2,1)S(1)}, u32[]{:S(2)}, u32[]{:S(2)}) collective-permute-start(s16[144,128]{1,0:T(8,128)(2,1)S(1)} %merge_hand.1.refs_0_), channel_id=1, source_target_pairs={{0,6},{2,4},{4,2},{6,0},{1,7},{3,5},{5,3},{7,1},{8,14},{10,12},{12... | collective-permute-start | bytes 110600 | tf_op jit(solution)/shard_map/ppermute | solution.py:502
  118.3 7.9 %collective-permute-start.6 = (s16[144,128]{1,0:T(8,128)(2,1)S(1)}, s16[144,128]{1,0:T(8,128)(2,1)S(1)}, u32[]{:S(2)}, u32[]{:S(2)}) collective-permute-start(s16[144,128]{1,0:T(8,128)(2,1)S(1)} %merge_hand.1.refs_0_), channel_id=1, source_target_pairs={{0,4},{2,6},{4,0},{6,2},{1,5},{3,7},{5,1},{7,3},{8,12},{10,14},{12... | collective-permute-start | bytes 110600 | tf_op jit(solution)/shard_map/ppermute | solution.py:502
  119.7 6.4 %collective-permute-start.5 = (s16[144,128]{1,0:T(8,128)(2,1)S(1)}, s16[144,128]{1,0:T(8,128)(2,1)S(1)}, u32[]{:S(2)}, u32[]{:S(2)}) collective-permute-start(s16[144,128]{1,0:T(8,128)(2,1)S(1)} %merge_hand.1.refs_0_), channel_id=1, source_target_pairs={{0,2},{2,0},{4,6},{6,4},{1,3},{3,1},{5,7},{7,5},{8,10},{10,8},{12,... | collective-permute-start | bytes 110600 | tf_op jit(solution)/shard_map/ppermute | solution.py:502

commit v3 on v2

--- a/solution.py
+++ b/solution.py
@@ -20,6 +20,7 @@
 QS = 8
 KS = 4
 NEWK = KS * TOK
+PIECE = 512
 TILE = 4 * TOK
 SCALE2 = HD**-0.5 * math.log2(math.e)
 NEG = -1e30
@@ -84,8 +85,9 @@
     return jnp.concatenate([ref[start : start + TOK, :] for ref in pairs], 0)
 
 
-def pack_query_kernel(meta, source, new_queries, dec_queries, out, rows):
-    upper = meta[0] > 0
+def pack_query_kernel(source, new_queries, dec_queries, out, rows):
+    tp, grp = lax.axis_index("tp"), lax.axis_index("grp")
+    upper = (tp & 1) > 0
     mine, blocks = [], []
     for r in range(4):
         wide = dec_queries[r].astype(f32)
@@ -95,7 +97,7 @@
         ]
         rows[r] = jnp.concatenate(heads, 0).astype(bf16)
         mine += [jnp.where(upper, heads[2 + j], heads[j]) for j in range(2)]
-        block = jnp.where(meta[1] > 0, source[r], -1).astype(f32)
+        block = jnp.where(grp == (tp >> 1), source[r], -1).astype(f32)
         blocks.append(jnp.full((16, HD), block, f32).astype(bf16))
     mine = jnp.concatenate(mine, 0).astype(bf16)
     blocks = jnp.concatenate(blocks, 0)
@@ -185,7 +187,9 @@
     for j, pair in enumerate(pairs):
         values_t[j] = values_of(pair)
     blocks = [
-        (functools.partial(keys_of, pairs[j]), lambda j=j: values_t[j], None) for j in range(EARLY)
+        (lambda j=j, n=n: pairs[j][n : n + PIECE, :], lambda j=j, n=n: values_t[j, :, n : n + PIECE], None)
+        for j in range(EARLY)
+        for n in range(0, CACHE, PIECE)
     ]
 
     def step(b, carry):
@@ -210,7 +214,7 @@
 
 def prefill_late_kernel(half, meta, queries, *refs):
     pairs = refs[:KS]
-    acc_in, sum_in, out, out_t, lse_all, values_t = refs[KS:]
+    acc_in, sum_in, out, lse_all, most_all, values_t = refs[KS:]
     new_keys = new_of(pairs, 0)
     new_values_t = new_of(pairs, 1).T
     for j in range(EARLY, KS):
@@ -226,6 +230,13 @@
         limit = token + meta[b] * TOK
         return jnp.concatenate([offset + meta[QS + j] * TOK <= limit for j in range(KS)], 0)
 
+    def put(b, acc, total, top):
+        most = jnp.maximum(jnp.max(jnp.abs(acc), 0, keepdims=True), 1e-30)
+        out[b, 0:HD, :] = jnp.round(acc * (CODE / most)).astype(i32).astype(i16)
+        size = jnp.log2(total)
+        lse_all[b] = size + top
+        most_all[b] = jnp.log2(most) - size
+
     def step(n, carry):
         places = [4 * n + k for k in range(4)]
         tiles = [tile_queries(queries, b, half) for b in places]
@@ -233,8 +244,7 @@
         states = [(sum_in[b], acc_in[b]) for b in places]
         for b, (total, acc) in zip(places, accumulate(tiles, states, cached + [new])):
             total = jnp.sum(total, 0, keepdims=True)
-            out_t[b] = acc / total
-            lse_all[b] = jnp.log2(total)
+            put(b, acc, total, 0.0)
         return carry
 
     lax.fori_loop(0, QS // 4, step, 0)
@@ -267,8 +277,7 @@
                 values = block[1]()
                 acc = acc * factor + matmul(values, first) + matmul(values, second)
                 top = new_top
-            out_t[b] = acc / total
-            lse_all[b] = jnp.log2(total) + top
+            put(b, acc, total, top)
             return carry
 
         lax.fori_loop(0, QS, one, 0)
@@ -276,10 +285,7 @@
     if half == 0:
         hand_sums = hand_off(meta, queries, pairs, out)
     for s in range(QS):
-        result = out_t[s]
-        most = jnp.maximum(jnp.max(jnp.abs(result), 0, keepdims=True), 1e-30)
-        out[s, 0:HD, :] = jnp.round(result * (CODE / most)).astype(i32).astype(i16)
-        words = [*two_words(lse_all[s]), *two_words(jnp.log2(most))]
+        words = [*two_words(lse_all[s]), *two_words(most_all[s])]
         words += hand_sums[s] if half == 0 else []
         words += [jnp.zeros((16 - len(words), TILE), f32)]
         out[s, HD : HD + 16, :] = jnp.concatenate(words, 0).astype(i32).astype(i16)
@@ -291,7 +297,7 @@
         "prefill_second" if half else "prefill_first",
         jax.ShapeDtypeStruct((QS, SECOND if half else FIRST, TILE), i16), 8,
         scratch=[
-            pltpu.VMEM((QS, HD, TILE), f32),
+            pltpu.VMEM((QS, 1, TILE), f32),
             pltpu.VMEM((QS, 1, TILE), f32),
             pltpu.VMEM((KS - EARLY, HD, CACHE), bf16),
         ],
@@ -400,26 +406,16 @@
         [part[0:HD], jnp.concatenate(blocks, 0)],
         [as_columns(part[HD:]), jnp.concatenate(lses, 0)],
     )
-    most = jnp.maximum(jnp.max(jnp.abs(result), 1, keepdims=True), 1e-30)
-    out[0:HD] = jnp.round(result * (CODE / most)).astype(i32).astype(i16)
-    wide = jnp.broadcast_to(jnp.log2(most), (HD, HD))
-    words = [*two_words(as_row(lse)[0:1]), *two_words(as_row(wide)[0:1]), jnp.zeros((12, HD), f32)]
-    out[HD:] = jnp.concatenate(words, 0).astype(i32).astype(i16)
+    out[0:HD] = result
+    out[HD:] = as_row(lse)
 
 
 def finish_kernel(meta, *refs):
     parts, (out, placed, rows) = refs[:4], refs[4:]
     for k in range(4):
         placed[meta[2] ^ k] = parts[k][...]
-    tails = [placed[t, HD:].astype(i32).astype(f32) for t in range(4)]
-    columns = jnp.concatenate(tails + [jnp.zeros((HD - 64, HD), f32)], 0).T
-    outs, lses = [], []
-    for t in range(4):
-        four = [columns[:, 16 * t + k : 16 * t + k + 1] for k in range(4)]
-        lses.append(one_number(four[0], four[1]))
-        scale = jnp.exp2(one_number(four[2], four[3])) / CODE
-        outs.append(placed[t, 0:HD].astype(i32).astype(f32) * scale)
-    rows[...] = merge(outs, lses)[0]
+    outs = [placed[t, 0:HD] for t in range(4)]
+    rows[...] = merge(outs, [as_columns(placed[t, HD:]) for t in range(4)])[0]
     for r in range(4):
         for g in range(GROUPS):
             lanes = slice(g * HD, (g + 1) * HD)
@@ -453,24 +449,24 @@
     def other_core(x):
         return lax.ppermute(x, "grp", [(0, 1), (1, 0)])
 
-    own_new = (new_keys[:, 0], new_values[:, 0])
-    pair = jnp.concatenate(
-        [cached_keys[:, 0], cached_values[:, 0], *own_new, *[other_core(x) for x in own_new]], 0
-    )
-
     def swap(x, bits):
         return lax.ppermute(x, "ctx", [(i, i ^ bits) for i in range(count)])
-
-    sent = [swap(pair, 16), swap(pair, 3)]
 
     holds = (grp == (tp >> 1)).astype(i32)
     flags = jnp.stack([tp & 1, holds, tp]).astype(i32)
     query, dec_queries = call(
         pack_query_kernel, "pack_query",
         [struct((QS, TOK, 10 * HD), bf16), struct((4, 32, HD), bf16)], 4,
-        in_specs=[SMEM] * 2 + [VMEM] * 2, out_specs=[VMEM] * 2, vmem=56 * 2**20,
-    )(flags, source_block, new_queries[:, 0], decode_queries)
+        in_specs=[SMEM] + [VMEM] * 2, out_specs=[VMEM] * 2, vmem=56 * 2**20,
+    )(source_block, new_queries[:, 0], decode_queries)
+    new_keys, new_values, query = lax.optimization_barrier((new_keys, new_values, query))
     queries = exchange(query)
+
+    own_new = (new_keys[:, 0], new_values[:, 0])
+    pair = jnp.concatenate(
+        [cached_keys[:, 0], cached_values[:, 0], *own_new, *[other_core(x) for x in own_new]], 0
+    )
+    sent = [swap(pair, 16), swap(pair, 3)]
 
     width = decode_keys.shape[1]
     live = decode_lengths - tp * width
@@ -481,12 +477,12 @@
         decode_values.reshape(4, width * 4, HD),
     )
 
+    later, part = lax.optimization_barrier((pair, part))
+    everyone = [pair, *sent, swap(later, 19)]
     queries, part = lax.optimization_barrier((queries, part))
     blocks = [(ctx & 18) + 4 * (k >> 1) + (k & 1) for k in range(QS)]
     blocks += [ctx ^ bits for bits in (0, 16, 3, 19)]
     meta = jnp.stack(blocks + [grp]).astype(i32)
-    later, *sent = lax.optimization_barrier((pair, *sent))
-    everyone = [pair, *sent, swap(later, 19)]
     acc0, acc1, sum0, sum1 = prefill_early(queries, everyone[:EARLY])
     first = prefill_late(0, meta, queries, everyone, acc0, sum0)
     meta, first = lax.optimization_barrier((meta, first))
@@ -496,7 +492,7 @@
 
     hand_back, second = lax.optimization_barrier((first_back, second))
     part = call(
-        merge_hand_kernel, "merge_hand", struct((HD + 16, HD), i16), 3,
+        merge_hand_kernel, "merge_hand", struct((HD + 8, HD), f32), 3,
         in_specs=[SMEM] + [VMEM] * 2, out_specs=VMEM,
     )(flags, part, hand_back)
     parts = [part] + [lax.ppermute(part, "tp", [(i, i ^ k) for i in range(4)]) for k in (1, 2, 3)]
@@ -506,7 +502,7 @@
     )(first_back, second_back)
     decode_out = call(
         finish_kernel, "finish", struct((4, 4, 8 * HD), bf16), 5,
-        scratch=[pltpu.VMEM((4, HD + 16, HD), i16), pltpu.VMEM((HD, HD), f32)],
+        scratch=[pltpu.VMEM((4, HD + 8, HD), f32), pltpu.VMEM((HD, HD), f32)],
         in_specs=[SMEM] + [VMEM] * 4, out_specs=VMEM,
     )(flags, *parts)
     return (out[:, None, :], decode_out)

time: 129 us -> 127 us (0.984)
  Pallas kernels: 76.6 us -> 74.6 us
    ppermute x3, waiting for transfers between devices: 6.67 us -> 0.76 us  [swap(): return lax.ppermute(x, 'ctx', [(i, i ^ bits) for i in range(count)])]
    all_to_all x3, waiting for transfers between devices: 1.24 us -> 6.4 us  [exchange(): return lax.all_to_all(x, 'ctx', 0, 0, axis_index_groups=groups, tiled=True)]
    unnamed x31 -> x29, local copies, waits for them, and re-layouts: 6.58 us -> 6.58 us
  transfers between devices with their start and end apart: 11 -> 11, of which waited for: 4 -> 4; matrix products, arithmetic and copies ran while one was open for 1% -> 0% of each run, Pallas kernels for 39% -> 36%
where the time goes in v3:
time: 127 us; the launch traced here: 126 us
  Pallas kernels  74.6 us (59%)
  starting transfers between devices  31.4 us (25%)
  waiting for transfers between devices  12.9 us (10%)
  local copies, waits for them, and re-layouts  6.67 us (5%)
    pallas_call x2, Pallas kernels, prefill_late(): call(functools.partial(prefill_late_kernel, half), 'prefill_second' if ha...  49.1 us
    all_to_all x3, starting transfers between devices, exchange(): return lax.all_to_all(x, 'ctx', 0, 0, axis_index_groups=groups, tiled=True)  18.4 us
    pallas_call x1, Pallas kernels, prefill_early(): call(prefill_early_kernel, 'prefill_early', outs, 1 + EARLY, scratch=[plt...  16.5 us
    ppermute x3, starting transfers between devices, local(): lax.ppermute(part, 'tp', [(i, i ^ k) for i in range(4)])  8.86 us
    unnamed x29, local copies, waits for them, and re-layouts  6.58 us
    all_to_all x3, waiting for transfers between devices, exchange(): return lax.all_to_all(x, 'ctx', 0, 0, axis_index_groups=groups, tiled=True)  6.4 us
    ppermute x3, waiting for transfers between devices, local(): lax.ppermute(part, 'tp', [(i, i ^ k) for i in range(4)])  5.01 us
    ppermute x3, starting transfers between devices, swap(): return lax.ppermute(x, 'ctx', [(i, i ^ bits) for i in range(count)])  3.64 us
  transfers between devices with their start and end apart: 11, of which 4 were waited for; matrix products, arithmetic and copies ran while one was open for 0% of the time, Pallas kernels for 36%

profile of v3, /device:TPU:8, one launch (start us, length us, event | category | flops | bytes accessed | tf_op | source)
XLA Modules:
  0.0 126.4 jit_solution(9357015012605463113)
XLA Ops:
  0.6 0.0 copy-start.10
  0.6 0.0 copy-start.9
  0.7 0.0 copy-start.7
  0.7 0.0 copy-start.8
  0.7 0.0 copy-start.11
  0.7 2.2 %pack_query.1 = (bf16[8,64,1280]{2,1,0:T(8,128)(2,1)}, bf16[4,32,128]{2,1,0:T(8,128)(2,1)}) custom-call(s32[4]{0:T(128)} %source.1, bf16[64,1024]{1,0:T(8,128)(2,1)} %bitcast.30, bf16[4,4,1024]{2,1,0:T(4,128)(2,1)} %dec_queries.1), custom_call_target="tpu_custom_call" | custom-call | flops 1000000 | bytes 500000 | tf_op jit(solution)/shard_map/pack_query/pallas_call | solution.py:457
  2.9 5.9 %all-to-all-start = ((bf16[8,64,1280]{2,1,0:T(8,128)(2,1)}), bf16[8,64,1280]{2,1,0:T(8,128)(2,1)S(1)}, u32[]{:S(2)}, u32[]{:S(2)}) async-start(bf16[8,64,1280]{2,1,0:T(8,128)(2,1)} %get-tuple-element.19), calls=%async_computation | async-start | bytes 2621440 | tf_op jit(solution)/shard_map/all_to_all | solution.py:447
  8.7 0.0 copy-done.10
  8.7 0.0 collective-permute-start.1
  8.7 0.0 copy-done.9
  8.8 0.5 collective-permute-start
  9.3 0.0 copy-done.7
  9.3 0.0 copy-done.8
  9.4 0.7 collective-permute-done
  10.1 0.0 collective-permute-done.1
  10.1 1.0 collective-permute-start.3
  11.1 1.9 %collective-permute-start.2 = (bf16[2304,128]{1,0:T(8,128)(2,1)S(1)}, bf16[2304,128]{1,0:T(8,128)(2,1)S(1)}, u32[]{:S(2)}, u32[]{:S(2)}) collective-permute-start(bf16[2304,128]{1,0:T(8,128)(2,1)S(1)} %constant_dynamic-update-slice_fusion.refs_0_), channel_id=1, source_target_pairs={{0,128},{8,136},{16,144},{24,152},{32,160},{40,168},{48,176},{56,1... | collective-permute-start | bytes 1769480 | tf_op jit(solution)/shard_map/ppermute | solution.py:453
  13.0 0.1 stack.70.meta
  13.1 0.0 copy-done.11
  13.2 0.0 copy-start
  13.2 1.6 %copy-done = bf16[4,512,4,128]{3,2,1,0:T(4,128)(2,1)S(1)} copy-done((bf16[4,512,4,128]{3,2,1,0:T(4,128)(2,1)S(1)}, bf16[4,512,4,128]{3,2,1,0:T(4,128)(2,1)}, u32[]{:S(2)}) %copy-start) | copy-done | bytes 2097176
  14.8 1.6 %copy-done.1 = bf16[4,512,4,128]{3,2,1,0:T(4,128)(2,1)S(1)} copy-done((bf16[4,512,4,128]{3,2,1,0:T(4,128)(2,1)S(1)}, bf16[4,512,4,128]{3,2,1,0:T(4,128)(2,1)}, u32[]{:S(2)}) %copy-start.1) | copy-done | bytes 2097176
  16.4 3.1 %decode_cache.1.part = f32[136,128]{1,0:T(8,128)S(1)} custom-call(s32[4]{0:T(128)S(1)} %broadcast_subtract_fusion.meta, bf16[4,32,128]{2,1,0:T(8,128)(2,1)S(1)} %copy-done.4, bf16[4,2048,128]{2,1,0:T(8,128)(2,1)S(1)} %bitcast.28, bf16[4,2048,128]{2,1,0:T(8,128)(2,1)S(1)} %bitcast.29), custom_call_target="tpu_custom_call" | custom-call | flops 2000000000 | bytes 4400000 | tf_op jit(solution)/shard_map/decode_cache/pallas_call | solution.py:366
  19.4 0.7 collective-permute-start.4
  20.1 6.4 %all-to-all-done.queries = bf16[8,64,1280]{2,1,0:T(8,128)(2,1)S(1)} async-done(((bf16[8,64,1280]{2,1,0:T(8,128)(2,1)}), bf16[8,64,1280]{2,1,0:T(8,128)(2,1)S(1)}, u32[]{:S(2)}, u32[]{:S(2)}) %all-to-all-start) | async-done | bytes 1310752 | tf_op jit(solution)/shard_map/all_to_all | solution.py:447
  26.5 0.0 collective-permute-done.3.refs_2_
  26.5 0.8 collective-permute-done.2.refs_1_
  27.3 16.5 %prefill_early.1 = (f32[8,128,256]{2,1,0:T(8,128)S(1)}, f32[8,128,256]{2,1,0:T(8,128)S(1)}, f32[8,8,256]{2,1,0:T(8,128)S(1)}, f32[8,8,256]{2,1,0:T(8,128)S(1)}) custom-call(bf16[8,64,1280]{2,1,0:T(8,128)(2,1)S(1)} %all-to-all-done.queries, bf16[2304,128]{1,0:T(8,128)(2,1)S(1)} %constant_dynamic-update-slice_fusion.refs_0_, ...), custom_call_target="tpu_custom_call" | custom-call | flops 9663676416 | bytes 4000000 | tf_op jit(solution)/shard_map/prefill_early/pallas_call | solution.py:208
  43.8 1.0 copy-done.5
  44.8 0.0 collective-permute-done.4.refs_3_
  44.8 25.0 %prefill_first.1 = s16[8,176,256]{2,1,0:T(8,128)(2,1)} custom-call(s32[13]{0:T(128)S(1)} %stack.70.meta, bf16[8,64,1280]{2,1,0:T(8,128)(2,1)S(1)} %all-to-all-done.queries, bf16[2304,128]{1,0:T(8,128)(2,1)S(1)} %constant_dynamic-update-slice_fusion.refs_0_, bf16[2304,128]{1,0:T(8,128)(2,1)S(1)} %collective-permute-done.2.refs_1_, ...), custom_call_target="tpu_custom_call" | custom-call | flops 2013265920 | bytes 4000000 | tf_op jit(solution)/shard_map/prefill_first/pallas_call | solution.py:295
  69.8 6.8 %all-to-all-start.1 = ((s16[8,176,256]{2,1,0:T(8,128)(2,1)}), s16[8,176,256]{2,1,0:T(8,128)(2,1)S(1)}, u32[]{:S(2)}, u32[]{:S(2)}) async-start(s16[8,176,256]{2,1,0:T(8,128)(2,1)} %prefill_first.1), calls=%async_computation.1 | async-start | bytes 1441792 | tf_op jit(solution)/shard_map/all_to_all | solution.py:447
  76.6 1.1 copy-done.3
  77.6 1.2 copy-done.6
  78.8 24.1 %prefill_second.1 = s16[8,144,256]{2,1,0:T(8,128)(2,1)} custom-call(s32[13]{0:T(128)S(1)} %stack.70.meta, bf16[8,64,1280]{2,1,0:T(8,128)(2,1)S(1)} %all-to-all-done.queries, bf16[2304,128]{1,0:T(8,128)(2,1)S(1)} %constant_dynamic-update-slice_fusion.refs_0_, bf16[2304,128]{1,0:T(8,128)(2,1)S(1)} %copy-done.3, ...), custom_call_target="tpu_custom_call" | custom-call | flops 2013265920 | bytes 4000000 | tf_op jit(solution)/shard_map/prefill_second/pallas_call | solution.py:295
  103.0 0.0 all-to-all-done.1.first.back
  103.0 5.7 %all-to-all-start.2 = ((s16[8,144,256]{2,1,0:T(8,128)(2,1)}), s16[8,144,256]{2,1,0:T(8,128)(2,1)S(1)}, u32[]{:S(2)}, u32[]{:S(2)}) async-start(s16[8,144,256]{2,1,0:T(8,128)(2,1)} %prefill_second.1), calls=%async_computation.2 | async-start | bytes 1179648 | tf_op jit(solution)/shard_map/all_to_all | solution.py:447
  108.7 0.1 pad_add_fusion.meta
  108.8 1.3 %merge_hand.1.refs_0_ = f32[136,128]{1,0:T(8,128)S(1)} custom-call(s32[3]{0:T(128)S(1)} %pad_add_fusion.meta, f32[136,128]{1,0:T(8,128)S(1)} %decode_cache.1.part, s16[8,176,256]{2,1,0:T(8,128)(2,1)S(1)} %all-to-all-done.1.first.back), custom_call_target="tpu_custom_call" | custom-call | flops 1000000 | bytes 500000 | tf_op jit(solution)/shard_map/merge_hand/pallas_call | solution.py:494
  110.1 6.4 %collective-permute-start.7 = (f32[136,128]{1,0:T(8,128)S(1)}, f32[136,128]{1,0:T(8,128)S(1)}, u32[]{:S(2)}, u32[]{:S(2)}) collective-permute-start(f32[136,128]{1,0:T(8,128)S(1)} %merge_hand.1.refs_0_), channel_id=1, source_target_pairs={{0,6},{2,4},{4,2},{6,0},{1,7},{3,5},{5,3},{7,1},{8,14},{10,12},{12... | collective-permute-start | bytes 208904 | tf_op jit(solution)/shard_map/ppermute | solution.py:498
  116.5 1.0 collective-permute-start.6
  117.5 1.5 %collective-permute-start.5 = (f32[136,128]{1,0:T(8,128)S(1)}, f32[136,128]{1,0:T(8,128)S(1)}, u32[]{:S(2)}, u32[]{:S(2)}) collective-permute-start(f32[136,128]{1,0:T(8,128)S(1)} %merge_hand.1.refs_0_), channel_id=1, source_target_pairs={{0,2},{2,0},{4,6},{6,4},{1,3},{3,1},{5,7},{7,5},{8,10},{10,8},{12,... | collective-permute-start | bytes 208904 | tf_op jit(solution)/shard_map/ppermute | solution.py:498
  119.0 0.0 all-to-all-done.2.second
  119.0 1.1 combine.1
  120.0 0.0 collective-permute-done.7.refs_3_
  120.0 5.0 %collective-permute-done.6.refs_2_ = f32[136,128]{1,0:T(8,128)S(1)} collective-permute-done((f32[136,128]{1,0:T(8,128)S(1)}, f32[136,128]{1,0:T(8,128)S(1)}, u32[]{:S(2)}, u32[]{:S(2)}) %collective-permute-start.6) | collective-permute-done | bytes 69664 | tf_op jit(solution)/shard_map/ppermute | solution.py:498
  125.0 0.0 collective-permute-done.5.refs_1_
  125.0 1.4 %finish.1 = bf16[4,4,1024]{2,1,0:T(4,128)(2,1)} custom-call(s32[3]{0:T(128)S(1)} %pad_add_fusion.meta, f32[136,128]{1,0:T(8,128)S(1)} %merge_hand.1.refs_0_, f32[136,128]{1,0:T(8,128)S(1)} %collective-permute-done.5.refs_1_, f32[136,128]{1,0:T(8,128)S(1)} %collective-permute-done.6.refs_2_, f32[136,128]{1,0:T(8,128)S(1)} %collective-permute-done.7.refs_3_), custom_call_target="tpu_custom_call" | custom-call | flops 1000000 | bytes 500000 | tf_op jit(solution)/shard_map/finish/pallas_call | solution.py:503
  (15 shorter events, 0.1 us)
Async XLA Ops:
  0.6 8.1 %copy-start.10 = (bf16[64,1,128]{2,0,1:T(8,128)(2,1)S(1)}, bf16[64,1,128]{2,0,1:T(8,128)(2,1)}, u32[]{:S(2)}) copy-start(bf16[64,1,128]{2,0,1:T(8,128)(2,1)} %param.12) | copy-start | bytes 49156
  0.6 8.1 %copy-start.9 = (bf16[64,1,128]{2,0,1:T(8,128)(2,1)S(1)}, bf16[64,1,128]{2,0,1:T(8,128)(2,1)}, u32[]{:S(2)}) copy-start(bf16[64,1,128]{2,0,1:T(8,128)(2,1)} %param.11) | copy-start | bytes 49156
  0.7 8.6 %copy-start.7 = (bf16[1024,1,128]{2,0,1:T(8,128)(2,1)S(1)}, bf16[1024,1,128]{2,0,1:T(8,128)(2,1)}, u32[]{:S(2)}) copy-start(bf16[1024,1,128]{2,0,1:T(8,128)(2,1)} %param.13) | copy-start | bytes 786436
  0.7 8.6 %copy-start.8 = (bf16[1024,1,128]{2,0,1:T(8,128)(2,1)S(1)}, bf16[1024,1,128]{2,0,1:T(8,128)(2,1)}, u32[]{:S(2)}) copy-start(bf16[1024,1,128]{2,0,1:T(8,128)(2,1)} %param.14) | copy-start | bytes 786436
  0.7 12.5 %copy-start.11 = (s32[4]{0:T(128)S(1)}, s32[4]{0:T(128)}, u32[]{:S(2)}) copy-start(s32[4]{0:T(128)} %param.18) | copy-start | bytes 52
  2.8 10.3 %copy-start.4 = (bf16[4,32,128]{2,1,0:T(8,128)(2,1)S(1)}, bf16[4,32,128]{2,1,0:T(8,128)(2,1)}, u32[]{:S(2)}) copy-start(bf16[4,32,128]{2,1,0:T(8,128)(2,1)} %get-tuple-element.22.q_ref) | copy-start | bytes 98308
  2.9 23.7 %all-to-all-start = ((bf16[8,64,1280]{2,1,0:T(8,128)(2,1)}), bf16[8,64,1280]{2,1,0:T(8,128)(2,1)S(1)}, u32[]{:S(2)}, u32[]{:S(2)}) async-start(bf16[8,64,1280]{2,1,0:T(8,128)(2,1)} %get-tuple-element.19), calls=%async_computation | async-start | bytes 2621440 | tf_op jit(solution)/shard_map/all_to_all | solution.py:447
  8.7 1.4 %collective-permute-start.1 = (bf16[64,128]{1,0:T(8,128)(2,1)S(1)}, bf16[64,128]{1,0:T(8,128)(2,1)S(1)}, u32[]{:S(2)}, u32[]{:S(2)}) collective-permute-start(bf16[64,128]{1,0:T(8,128)(2,1)S(1)} %bitcast.32), channel_id=1, source_target_pairs={{0,1},{1,0},{2,3},{3,2},{4,5},{5,4},{6,7},{7,6},{8,9},{9,8},{10,11... | collective-permute-start | bytes 49160 | tf_op jit(solution)/shard_map/ppermute | solution.py:450
  8.8 1.3 %collective-permute-start = (bf16[64,128]{1,0:T(8,128)(2,1)S(1)}, bf16[64,128]{1,0:T(8,128)(2,1)S(1)}, u32[]{:S(2)}, u32[]{:S(2)}) collective-permute-start(bf16[64,128]{1,0:T(8,128)(2,1)S(1)} %bitcast.31), channel_id=1, source_target_pairs={{0,1},{1,0},{2,3},{3,2},{4,5},{5,4},{6,7},{7,6},{8,9},{9,8},{10,11... | collective-permute-start | bytes 49160 | tf_op jit(solution)/shard_map/ppermute | solution.py:450
  10.1 16.4 %collective-permute-start.3 = (bf16[2304,128]{1,0:T(8,128)(2,1)S(1)}, bf16[2304,128]{1,0:T(8,128)(2,1)S(1)}, u32[]{:S(2)}, u32[]{:S(2)}) collective-permute-start(bf16[2304,128]{1,0:T(8,128)(2,1)S(1)} %constant_dynamic-update-slice_fusion.refs_0_), channel_id=1, source_target_pairs={{0,24},{8,16},{16,8},{24,0},{32,56},{40,48},{48,40},{56,32},{64,88... | collective-permute-start | bytes 1769480 | tf_op jit(solution)/shard_map/ppermute | solution.py:453
  11.1 16.2 %collective-permute-start.2 = (bf16[2304,128]{1,0:T(8,128)(2,1)S(1)}, bf16[2304,128]{1,0:T(8,128)(2,1)S(1)}, u32[]{:S(2)}, u32[]{:S(2)}) collective-permute-start(bf16[2304,128]{1,0:T(8,128)(2,1)S(1)} %constant_dynamic-update-slice_fusion.refs_0_), channel_id=1, source_target_pairs={{0,128},{8,136},{16,144},{24,152},{32,160},{40,168},{48,176},{56,1... | collective-permute-start | bytes 1769480 | tf_op jit(solution)/shard_map/ppermute | solution.py:453
  13.2 1.6 %copy-start = (bf16[4,512,4,128]{3,2,1,0:T(4,128)(2,1)S(1)}, bf16[4,512,4,128]{3,2,1,0:T(4,128)(2,1)}, u32[]{:S(2)}) copy-start(bf16[4,512,4,128]{3,2,1,0:T(4,128)(2,1)} %param.16) | copy-start | bytes 6291460
  14.8 1.6 %copy-start.1 = (bf16[4,512,4,128]{3,2,1,0:T(4,128)(2,1)S(1)}, bf16[4,512,4,128]{3,2,1,0:T(4,128)(2,1)}, u32[]{:S(2)}) copy-start(bf16[4,512,4,128]{3,2,1,0:T(4,128)(2,1)} %param.17) | copy-start | bytes 6291460
  19.4 25.4 %collective-permute-start.4 = (bf16[2304,128]{1,0:T(8,128)(2,1)S(1)}, bf16[2304,128]{1,0:T(8,128)(2,1)}, u32[]{:S(2)}, u32[]{:S(2)}) collective-permute-start(bf16[2304,128]{1,0:T(8,128)(2,1)S(1)} %constant_dynamic-update-slice_fusion.refs_0_), channel_id=1, source_target_pairs={{0,152},{8,144},{16,136},{24,128},{32,184},{40,176},{48,168},{56,1... | collective-permute-start | bytes 1769480 | tf_op jit(solution)/shard_map/ppermute | solution.py:453
  27.3 17.5 %copy-start.2 = (bf16[2304,128]{1,0:T(8,128)(2,1)}, bf16[2304,128]{1,0:T(8,128)(2,1)S(1)}, u32[]{:S(2)}) copy-start(bf16[2304,128]{1,0:T(8,128)(2,1)S(1)} %collective-permute-done.2.refs_1_) | copy-start | bytes 1769476
  43.8 1.0 copy-start.5
  69.8 33.2 %all-to-all-start.1 = ((s16[8,176,256]{2,1,0:T(8,128)(2,1)}), s16[8,176,256]{2,1,0:T(8,128)(2,1)S(1)}, u32[]{:S(2)}, u32[]{:S(2)}) async-start(s16[8,176,256]{2,1,0:T(8,128)(2,1)} %prefill_first.1), calls=%async_computation.1 | async-start | bytes 1441792 | tf_op jit(solution)/shard_map/all_to_all | solution.py:447
  76.6 1.1 copy-start.3
  77.6 1.2 copy-start.6
  103.0 16.0 %all-to-all-start.2 = ((s16[8,144,256]{2,1,0:T(8,128)(2,1)}), s16[8,144,256]{2,1,0:T(8,128)(2,1)S(1)}, u32[]{:S(2)}, u32[]{:S(2)}) async-start(s16[8,144,256]{2,1,0:T(8,128)(2,1)} %prefill_second.1), calls=%async_computation.2 | async-start | bytes 1179648 | tf_op jit(solution)/shard_map/all_to_all | solution.py:447
  110.1 9.9 %collective-permute-start.7 = (f32[136,128]{1,0:T(8,128)S(1)}, f32[136,128]{1,0:T(8,128)S(1)}, u32[]{:S(2)}, u32[]{:S(2)}) collective-permute-start(f32[136,128]{1,0:T(8,128)S(1)} %merge_hand.1.refs_0_), channel_id=1, source_target_pairs={{0,6},{2,4},{4,2},{6,0},{1,7},{3,5},{5,3},{7,1},{8,14},{10,12},{12... | collective-permute-start | bytes 208904 | tf_op jit(solution)/shard_map/ppermute | solution.py:498
  116.5 8.5 %collective-permute-start.6 = (f32[136,128]{1,0:T(8,128)S(1)}, f32[136,128]{1,0:T(8,128)S(1)}, u32[]{:S(2)}, u32[]{:S(2)}) collective-permute-start(f32[136,128]{1,0:T(8,128)S(1)} %merge_hand.1.refs_0_), channel_id=1, source_target_pairs={{0,4},{2,6},{4,0},{6,2},{1,5},{3,7},{5,1},{7,3},{8,12},{10,14},{12... | collective-permute-start | bytes 208904 | tf_op jit(solution)/shard_map/ppermute | solution.py:498
  117.5 7.6 %collective-permute-start.5 = (f32[136,128]{1,0:T(8,128)S(1)}, f32[136,128]{1,0:T(8,128)S(1)}, u32[]{:S(2)}, u32[]{:S(2)}) collective-permute-start(f32[136,128]{1,0:T(8,128)S(1)} %merge_hand.1.refs_0_), channel_id=1, source_target_pairs={{0,2},{2,0},{4,6},{6,4},{1,3},{3,1},{5,7},{7,5},{8,10},{10,8},{12,... | collective-permute-start | bytes 208904 | tf_op jit(solution)/shard_map/ppermute | solution.py:498

commit v4 on v3

--- a/solution.py
+++ b/solution.py
@@ -220,8 +220,13 @@
     for j in range(EARLY, KS):
         values_t[j - EARLY] = values_of(pairs[j])
     cached = [
-        (functools.partial(keys_of, pairs[j]), lambda j=j: values_t[j - EARLY], None)
+        (
+            lambda j=j, n=n: pairs[j][n : n + PIECE, :],
+            lambda j=j, n=n: values_t[j - EARLY, :, n : n + PIECE],
+            None,
+        )
         for j in range(EARLY, KS)
+        for n in range(0, CACHE, PIECE)
     ]
 
     def allowed(b):

time: 127 us -> 127 us (level)
  no operation moved by 1% of the time
where the time goes in v4:
time: 127 us; the launch traced here: 126 us
  Pallas kernels  74.2 us (58%)
  starting transfers between devices  31.4 us (25%)
  waiting for transfers between devices  12.9 us (10%)
  local copies, waits for them, and re-layouts  6.67 us (5%)
    pallas_call x2, Pallas kernels, prefill_late(): call(functools.partial(prefill_late_kernel, half), 'prefill_second' if ha...  48.7 us
    all_to_all x3, starting transfers between devices, exchange(): return lax.all_to_all(x, 'ctx', 0, 0, axis_index_groups=groups, tiled=True)  18.4 us
    pallas_call x1, Pallas kernels, prefill_early(): call(prefill_early_kernel, 'prefill_early', outs, 1 + EARLY, scratch=[plt...  16.5 us
    ppermute x3, starting transfers between devices, local(): lax.ppermute(part, 'tp', [(i, i ^ k) for i in range(4)])  8.86 us
    unnamed x29, local copies, waits for them, and re-layouts  6.58 us
    all_to_all x3, waiting for transfers between devices, exchange(): return lax.all_to_all(x, 'ctx', 0, 0, axis_index_groups=groups, tiled=True)  6.4 us
    ppermute x3, waiting for transfers between devices, local(): lax.ppermute(part, 'tp', [(i, i ^ k) for i in range(4)])  5.01 us
    ppermute x3, starting transfers between devices, swap(): return lax.ppermute(x, 'ctx', [(i, i ^ bits) for i in range(count)])  3.64 us
  transfers between devices with their start and end apart: 11, of which 4 were waited for; matrix products, arithmetic and copies ran while one was open for 0% of the time, Pallas kernels for 36%

profile of v4, /device:TPU:8, one launch (start us, length us, event | category | flops | bytes accessed | tf_op | source)
XLA Modules:
  0.0 126.0 jit_solution(15982161121142020881)
XLA Ops:
  0.6 0.0 copy-start.10
  0.6 0.0 copy-start.9
  0.7 0.0 copy-start.7
  0.7 0.0 copy-start.8
  0.7 0.0 copy-start.11
  0.7 2.2 %pack_query.1 = (bf16[8,64,1280]{2,1,0:T(8,128)(2,1)}, bf16[4,32,128]{2,1,0:T(8,128)(2,1)}) custom-call(s32[4]{0:T(128)} %source.1, bf16[64,1024]{1,0:T(8,128)(2,1)} %bitcast.30, bf16[4,4,1024]{2,1,0:T(4,128)(2,1)} %dec_queries.1), custom_call_target="tpu_custom_call" | custom-call | flops 1000000 | bytes 500000 | tf_op jit(solution)/shard_map/pack_query/pallas_call | solution.py:462
  2.9 5.9 %all-to-all-start = ((bf16[8,64,1280]{2,1,0:T(8,128)(2,1)}), bf16[8,64,1280]{2,1,0:T(8,128)(2,1)S(1)}, u32[]{:S(2)}, u32[]{:S(2)}) async-start(bf16[8,64,1280]{2,1,0:T(8,128)(2,1)} %get-tuple-element.19), calls=%async_computation | async-start | bytes 2621440 | tf_op jit(solution)/shard_map/all_to_all | solution.py:452
  8.7 0.0 copy-done.10
  8.7 0.0 collective-permute-start.1
  8.7 0.0 copy-done.9
  8.8 0.5 collective-permute-start
  9.3 0.0 copy-done.7
  9.3 0.0 copy-done.8
  9.4 0.7 collective-permute-done
  10.1 0.0 collective-permute-done.1
  10.1 1.0 collective-permute-start.3
  11.1 1.9 %collective-permute-start.2 = (bf16[2304,128]{1,0:T(8,128)(2,1)S(1)}, bf16[2304,128]{1,0:T(8,128)(2,1)S(1)}, u32[]{:S(2)}, u32[]{:S(2)}) collective-permute-start(bf16[2304,128]{1,0:T(8,128)(2,1)S(1)} %constant_dynamic-update-slice_fusion.refs_0_), channel_id=1, source_target_pairs={{0,128},{8,136},{16,144},{24,152},{32,160},{40,168},{48,176},{56,1... | collective-permute-start | bytes 1769480 | tf_op jit(solution)/shard_map/ppermute | solution.py:458
  13.0 0.1 stack.70.meta
  13.1 0.0 copy-done.11
  13.2 0.0 copy-start
  13.2 1.6 %copy-done = bf16[4,512,4,128]{3,2,1,0:T(4,128)(2,1)S(1)} copy-done((bf16[4,512,4,128]{3,2,1,0:T(4,128)(2,1)S(1)}, bf16[4,512,4,128]{3,2,1,0:T(4,128)(2,1)}, u32[]{:S(2)}) %copy-start) | copy-done | bytes 2097176
  14.8 1.6 %copy-done.1 = bf16[4,512,4,128]{3,2,1,0:T(4,128)(2,1)S(1)} copy-done((bf16[4,512,4,128]{3,2,1,0:T(4,128)(2,1)S(1)}, bf16[4,512,4,128]{3,2,1,0:T(4,128)(2,1)}, u32[]{:S(2)}) %copy-start.1) | copy-done | bytes 2097176
  16.4 3.1 %decode_cache.1.part = f32[136,128]{1,0:T(8,128)S(1)} custom-call(s32[4]{0:T(128)S(1)} %broadcast_subtract_fusion.meta, bf16[4,32,128]{2,1,0:T(8,128)(2,1)S(1)} %copy-done.4, bf16[4,2048,128]{2,1,0:T(8,128)(2,1)S(1)} %bitcast.28, bf16[4,2048,128]{2,1,0:T(8,128)(2,1)S(1)} %bitcast.29), custom_call_target="tpu_custom_call" | custom-call | flops 2000000000 | bytes 4400000 | tf_op jit(solution)/shard_map/decode_cache/pallas_call | solution.py:371
  19.4 0.7 collective-permute-start.4
  20.1 6.4 %all-to-all-done.queries = bf16[8,64,1280]{2,1,0:T(8,128)(2,1)S(1)} async-done(((bf16[8,64,1280]{2,1,0:T(8,128)(2,1)}), bf16[8,64,1280]{2,1,0:T(8,128)(2,1)S(1)}, u32[]{:S(2)}, u32[]{:S(2)}) %all-to-all-start) | async-done | bytes 1310752 | tf_op jit(solution)/shard_map/all_to_all | solution.py:452
  26.5 0.0 collective-permute-done.3.refs_2_
  26.5 0.8 collective-permute-done.2.refs_1_
  27.3 16.5 %prefill_early.1 = (f32[8,128,256]{2,1,0:T(8,128)S(1)}, f32[8,128,256]{2,1,0:T(8,128)S(1)}, f32[8,8,256]{2,1,0:T(8,128)S(1)}, f32[8,8,256]{2,1,0:T(8,128)S(1)}) custom-call(bf16[8,64,1280]{2,1,0:T(8,128)(2,1)S(1)} %all-to-all-done.queries, bf16[2304,128]{1,0:T(8,128)(2,1)S(1)} %constant_dynamic-update-slice_fusion.refs_0_, ...), custom_call_target="tpu_custom_call" | custom-call | flops 9663676416 | bytes 4000000 | tf_op jit(solution)/shard_map/prefill_early/pallas_call | solution.py:208
  43.8 1.0 copy-done.5
  44.8 0.0 collective-permute-done.4.refs_3_
  44.8 24.8 %prefill_first.1 = s16[8,176,256]{2,1,0:T(8,128)(2,1)} custom-call(s32[13]{0:T(128)S(1)} %stack.70.meta, bf16[8,64,1280]{2,1,0:T(8,128)(2,1)S(1)} %all-to-all-done.queries, bf16[2304,128]{1,0:T(8,128)(2,1)S(1)} %constant_dynamic-update-slice_fusion.refs_0_, bf16[2304,128]{1,0:T(8,128)(2,1)S(1)} %collective-permute-done.2.refs_1_, ...), custom_call_target="tpu_custom_call" | custom-call | flops 2013265920 | bytes 4000000 | tf_op jit(solution)/shard_map/prefill_first/pallas_call | solution.py:300
  69.6 6.8 %all-to-all-start.1 = ((s16[8,176,256]{2,1,0:T(8,128)(2,1)}), s16[8,176,256]{2,1,0:T(8,128)(2,1)S(1)}, u32[]{:S(2)}, u32[]{:S(2)}) async-start(s16[8,176,256]{2,1,0:T(8,128)(2,1)} %prefill_first.1), calls=%async_computation.1 | async-start | bytes 1441792 | tf_op jit(solution)/shard_map/all_to_all | solution.py:452
  76.4 1.1 copy-done.3
  77.4 1.2 copy-done.6
  78.6 23.9 %prefill_second.1 = s16[8,144,256]{2,1,0:T(8,128)(2,1)} custom-call(s32[13]{0:T(128)S(1)} %stack.70.meta, bf16[8,64,1280]{2,1,0:T(8,128)(2,1)S(1)} %all-to-all-done.queries, bf16[2304,128]{1,0:T(8,128)(2,1)S(1)} %constant_dynamic-update-slice_fusion.refs_0_, bf16[2304,128]{1,0:T(8,128)(2,1)S(1)} %copy-done.3, ...), custom_call_target="tpu_custom_call" | custom-call | flops 2013265920 | bytes 4000000 | tf_op jit(solution)/shard_map/prefill_second/pallas_call | solution.py:300
  102.6 0.0 all-to-all-done.1.first.back
  102.6 5.7 %all-to-all-start.2 = ((s16[8,144,256]{2,1,0:T(8,128)(2,1)}), s16[8,144,256]{2,1,0:T(8,128)(2,1)S(1)}, u32[]{:S(2)}, u32[]{:S(2)}) async-start(s16[8,144,256]{2,1,0:T(8,128)(2,1)} %prefill_second.1), calls=%async_computation.2 | async-start | bytes 1179648 | tf_op jit(solution)/shard_map/all_to_all | solution.py:452
  108.3 0.1 pad_add_fusion.meta
  108.4 1.3 %merge_hand.1.refs_0_ = f32[136,128]{1,0:T(8,128)S(1)} custom-call(s32[3]{0:T(128)S(1)} %pad_add_fusion.meta, f32[136,128]{1,0:T(8,128)S(1)} %decode_cache.1.part, s16[8,176,256]{2,1,0:T(8,128)(2,1)S(1)} %all-to-all-done.1.first.back), custom_call_target="tpu_custom_call" | custom-call | flops 1000000 | bytes 500000 | tf_op jit(solution)/shard_map/merge_hand/pallas_call | solution.py:499
  109.7 6.4 %collective-permute-start.7 = (f32[136,128]{1,0:T(8,128)S(1)}, f32[136,128]{1,0:T(8,128)S(1)}, u32[]{:S(2)}, u32[]{:S(2)}) collective-permute-start(f32[136,128]{1,0:T(8,128)S(1)} %merge_hand.1.refs_0_), channel_id=1, source_target_pairs={{0,6},{2,4},{4,2},{6,0},{1,7},{3,5},{5,3},{7,1},{8,14},{10,12},{12... | collective-permute-start | bytes 208904 | tf_op jit(solution)/shard_map/ppermute | solution.py:503
  116.1 1.0 collective-permute-start.6
  117.1 1.5 %collective-permute-start.5 = (f32[136,128]{1,0:T(8,128)S(1)}, f32[136,128]{1,0:T(8,128)S(1)}, u32[]{:S(2)}, u32[]{:S(2)}) collective-permute-start(f32[136,128]{1,0:T(8,128)S(1)} %merge_hand.1.refs_0_), channel_id=1, source_target_pairs={{0,2},{2,0},{4,6},{6,4},{1,3},{3,1},{5,7},{7,5},{8,10},{10,8},{12,... | collective-permute-start | bytes 208904 | tf_op jit(solution)/shard_map/ppermute | solution.py:503
  118.6 0.0 all-to-all-done.2.second
  118.6 1.1 combine.1
  119.6 0.0 collective-permute-done.7.refs_3_
  119.6 5.0 %collective-permute-done.6.refs_2_ = f32[136,128]{1,0:T(8,128)S(1)} collective-permute-done((f32[136,128]{1,0:T(8,128)S(1)}, f32[136,128]{1,0:T(8,128)S(1)}, u32[]{:S(2)}, u32[]{:S(2)}) %collective-permute-start.6) | collective-permute-done | bytes 69664 | tf_op jit(solution)/shard_map/ppermute | solution.py:503
  124.6 0.0 collective-permute-done.5.refs_1_
  124.7 1.4 %finish.1 = bf16[4,4,1024]{2,1,0:T(4,128)(2,1)} custom-call(s32[3]{0:T(128)S(1)} %pad_add_fusion.meta, f32[136,128]{1,0:T(8,128)S(1)} %merge_hand.1.refs_0_, f32[136,128]{1,0:T(8,128)S(1)} %collective-permute-done.5.refs_1_, f32[136,128]{1,0:T(8,128)S(1)} %collective-permute-done.6.refs_2_, f32[136,128]{1,0:T(8,128)S(1)} %collective-permute-done.7.refs_3_), custom_call_target="tpu_custom_call" | custom-call | flops 1000000 | bytes 500000 | tf_op jit(solution)/shard_map/finish/pallas_call | solution.py:508
  (15 shorter events, 0.1 us)
Async XLA Ops:
  0.6 8.1 %copy-start.10 = (bf16[64,1,128]{2,0,1:T(8,128)(2,1)S(1)}, bf16[64,1,128]{2,0,1:T(8,128)(2,1)}, u32[]{:S(2)}) copy-start(bf16[64,1,128]{2,0,1:T(8,128)(2,1)} %param.12) | copy-start | bytes 49156
  0.6 8.1 %copy-start.9 = (bf16[64,1,128]{2,0,1:T(8,128)(2,1)S(1)}, bf16[64,1,128]{2,0,1:T(8,128)(2,1)}, u32[]{:S(2)}) copy-start(bf16[64,1,128]{2,0,1:T(8,128)(2,1)} %param.11) | copy-start | bytes 49156
  0.7 8.6 %copy-start.7 = (bf16[1024,1,128]{2,0,1:T(8,128)(2,1)S(1)}, bf16[1024,1,128]{2,0,1:T(8,128)(2,1)}, u32[]{:S(2)}) copy-start(bf16[1024,1,128]{2,0,1:T(8,128)(2,1)} %param.13) | copy-start | bytes 786436
  0.7 8.6 %copy-start.8 = (bf16[1024,1,128]{2,0,1:T(8,128)(2,1)S(1)}, bf16[1024,1,128]{2,0,1:T(8,128)(2,1)}, u32[]{:S(2)}) copy-start(bf16[1024,1,128]{2,0,1:T(8,128)(2,1)} %param.14) | copy-start | bytes 786436
  0.7 12.5 %copy-start.11 = (s32[4]{0:T(128)S(1)}, s32[4]{0:T(128)}, u32[]{:S(2)}) copy-start(s32[4]{0:T(128)} %param.18) | copy-start | bytes 52
  2.8 10.3 %copy-start.4 = (bf16[4,32,128]{2,1,0:T(8,128)(2,1)S(1)}, bf16[4,32,128]{2,1,0:T(8,128)(2,1)}, u32[]{:S(2)}) copy-start(bf16[4,32,128]{2,1,0:T(8,128)(2,1)} %get-tuple-element.22.q_ref) | copy-start | bytes 98308
  2.9 23.7 %all-to-all-start = ((bf16[8,64,1280]{2,1,0:T(8,128)(2,1)}), bf16[8,64,1280]{2,1,0:T(8,128)(2,1)S(1)}, u32[]{:S(2)}, u32[]{:S(2)}) async-start(bf16[8,64,1280]{2,1,0:T(8,128)(2,1)} %get-tuple-element.19), calls=%async_computation | async-start | bytes 2621440 | tf_op jit(solution)/shard_map/all_to_all | solution.py:452
  8.7 1.4 %collective-permute-start.1 = (bf16[64,128]{1,0:T(8,128)(2,1)S(1)}, bf16[64,128]{1,0:T(8,128)(2,1)S(1)}, u32[]{:S(2)}, u32[]{:S(2)}) collective-permute-start(bf16[64,128]{1,0:T(8,128)(2,1)S(1)} %bitcast.32), channel_id=1, source_target_pairs={{0,1},{1,0},{2,3},{3,2},{4,5},{5,4},{6,7},{7,6},{8,9},{9,8},{10,11... | collective-permute-start | bytes 49160 | tf_op jit(solution)/shard_map/ppermute | solution.py:455
  8.8 1.3 %collective-permute-start = (bf16[64,128]{1,0:T(8,128)(2,1)S(1)}, bf16[64,128]{1,0:T(8,128)(2,1)S(1)}, u32[]{:S(2)}, u32[]{:S(2)}) collective-permute-start(bf16[64,128]{1,0:T(8,128)(2,1)S(1)} %bitcast.31), channel_id=1, source_target_pairs={{0,1},{1,0},{2,3},{3,2},{4,5},{5,4},{6,7},{7,6},{8,9},{9,8},{10,11... | collective-permute-start | bytes 49160 | tf_op jit(solution)/shard_map/ppermute | solution.py:455
  10.1 16.4 %collective-permute-start.3 = (bf16[2304,128]{1,0:T(8,128)(2,1)S(1)}, bf16[2304,128]{1,0:T(8,128)(2,1)S(1)}, u32[]{:S(2)}, u32[]{:S(2)}) collective-permute-start(bf16[2304,128]{1,0:T(8,128)(2,1)S(1)} %constant_dynamic-update-slice_fusion.refs_0_), channel_id=1, source_target_pairs={{0,24},{8,16},{16,8},{24,0},{32,56},{40,48},{48,40},{56,32},{64,88... | collective-permute-start | bytes 1769480 | tf_op jit(solution)/shard_map/ppermute | solution.py:458
  11.1 16.2 %collective-permute-start.2 = (bf16[2304,128]{1,0:T(8,128)(2,1)S(1)}, bf16[2304,128]{1,0:T(8,128)(2,1)S(1)}, u32[]{:S(2)}, u32[]{:S(2)}) collective-permute-start(bf16[2304,128]{1,0:T(8,128)(2,1)S(1)} %constant_dynamic-update-slice_fusion.refs_0_), channel_id=1, source_target_pairs={{0,128},{8,136},{16,144},{24,152},{32,160},{40,168},{48,176},{56,1... | collective-permute-start | bytes 1769480 | tf_op jit(solution)/shard_map/ppermute | solution.py:458
  13.2 1.6 %copy-start = (bf16[4,512,4,128]{3,2,1,0:T(4,128)(2,1)S(1)}, bf16[4,512,4,128]{3,2,1,0:T(4,128)(2,1)}, u32[]{:S(2)}) copy-start(bf16[4,512,4,128]{3,2,1,0:T(4,128)(2,1)} %param.16) | copy-start | bytes 6291460
  14.8 1.6 %copy-start.1 = (bf16[4,512,4,128]{3,2,1,0:T(4,128)(2,1)S(1)}, bf16[4,512,4,128]{3,2,1,0:T(4,128)(2,1)}, u32[]{:S(2)}) copy-start(bf16[4,512,4,128]{3,2,1,0:T(4,128)(2,1)} %param.17) | copy-start | bytes 6291460
  19.4 25.4 %collective-permute-start.4 = (bf16[2304,128]{1,0:T(8,128)(2,1)S(1)}, bf16[2304,128]{1,0:T(8,128)(2,1)}, u32[]{:S(2)}, u32[]{:S(2)}) collective-permute-start(bf16[2304,128]{1,0:T(8,128)(2,1)S(1)} %constant_dynamic-update-slice_fusion.refs_0_), channel_id=1, source_target_pairs={{0,152},{8,144},{16,136},{24,128},{32,184},{40,176},{48,168},{56,1... | collective-permute-start | bytes 1769480 | tf_op jit(solution)/shard_map/ppermute | solution.py:458
  27.3 17.5 %copy-start.2 = (bf16[2304,128]{1,0:T(8,128)(2,1)}, bf16[2304,128]{1,0:T(8,128)(2,1)S(1)}, u32[]{:S(2)}) copy-start(bf16[2304,128]{1,0:T(8,128)(2,1)S(1)} %collective-permute-done.2.refs_1_) | copy-start | bytes 1769476
  43.8 1.0 copy-start.5
  69.6 33.0 %all-to-all-start.1 = ((s16[8,176,256]{2,1,0:T(8,128)(2,1)}), s16[8,176,256]{2,1,0:T(8,128)(2,1)S(1)}, u32[]{:S(2)}, u32[]{:S(2)}) async-start(s16[8,176,256]{2,1,0:T(8,128)(2,1)} %prefill_first.1), calls=%async_computation.1 | async-start | bytes 1441792 | tf_op jit(solution)/shard_map/all_to_all | solution.py:452
  76.4 1.1 copy-start.3
  77.4 1.2 copy-start.6
  102.6 16.0 %all-to-all-start.2 = ((s16[8,144,256]{2,1,0:T(8,128)(2,1)}), s16[8,144,256]{2,1,0:T(8,128)(2,1)S(1)}, u32[]{:S(2)}, u32[]{:S(2)}) async-start(s16[8,144,256]{2,1,0:T(8,128)(2,1)} %prefill_second.1), calls=%async_computation.2 | async-start | bytes 1179648 | tf_op jit(solution)/shard_map/all_to_all | solution.py:452
  109.7 9.9 %collective-permute-start.7 = (f32[136,128]{1,0:T(8,128)S(1)}, f32[136,128]{1,0:T(8,128)S(1)}, u32[]{:S(2)}, u32[]{:S(2)}) collective-permute-start(f32[136,128]{1,0:T(8,128)S(1)} %merge_hand.1.refs_0_), channel_id=1, source_target_pairs={{0,6},{2,4},{4,2},{6,0},{1,7},{3,5},{5,3},{7,1},{8,14},{10,12},{12... | collective-permute-start | bytes 208904 | tf_op jit(solution)/shard_map/ppermute | solution.py:503
  116.1 8.5 %collective-permute-start.6 = (f32[136,128]{1,0:T(8,128)S(1)}, f32[136,128]{1,0:T(8,128)S(1)}, u32[]{:S(2)}, u32[]{:S(2)}) collective-permute-start(f32[136,128]{1,0:T(8,128)S(1)} %merge_hand.1.refs_0_), channel_id=1, source_target_pairs={{0,4},{2,6},{4,0},{6,2},{1,5},{3,7},{5,1},{7,3},{8,12},{10,14},{12... | collective-permute-start | bytes 208904 | tf_op jit(solution)/shard_map/ppermute | solution.py:503
  117.1 7.6 %collective-permute-start.5 = (f32[136,128]{1,0:T(8,128)S(1)}, f32[136,128]{1,0:T(8,128)S(1)}, u32[]{:S(2)}, u32[]{:S(2)}) collective-permute-start(f32[136,128]{1,0:T(8,128)S(1)} %merge_hand.1.refs_0_), channel_id=1, source_target_pairs={{0,2},{2,0},{4,6},{6,4},{1,3},{3,1},{5,7},{7,5},{8,10},{10,8},{12,... | collective-permute-start | bytes 208904 | tf_op jit(solution)/shard_map/ppermute | solution.py:503
